TPU v7x, 32 devices: a whole 2x2x4 slice. The times are simulated.
32 devices in a mesh: region: 2 (over y), member: 16 (over z, x, core).
Axes of the slice: x: 2, y: 2, z: 4, core: 2. Of those that a mesh axis runs over, the one named last changes fastest.
Arguments:
- perm_prior: float32 [128, 64, 512], P(('region', 'member')), parts along dimension 0, may hold values from -1.5 to 1.5
- start_height: float32 [128, 512], P('region'), parts along dimension 0, may hold values from 0.2 to 1
- top_surface: float32 [128, 512], P('region'), parts along dimension 0, may hold values from 0 to 0.5
- porosity: float32 [128, 512], P('region'), parts along dimension 0, may hold values from 0.15 to 0.3
- well_mask: int32 [128, 512], P('region'), parts along dimension 0, may hold values 0 or 1
- obs_cells: int32 [4, 128], P('region'), parts along dimension 0, may hold values from 0 to 32767
- observed: float32 [4, 128], P('region'), parts along dimension 0, may hold values from -0.3 to 0.3
- obs_error: float32 [256], P('region'), parts along dimension 0, may hold values from 0.03 to 0.06
- noise_table: int32 [4, 64, 128], P('region', 'member'), parts along dimension 0, may hold values from 0 to 255
Outputs:
- perm_post: float32 [128, 64, 512], P(('region', 'member')), parts along dimension 0
There are 2 independent parts, one for each index of `region`. A program takes and returns all parts, laid end to end along the dimension named above; each array names one. Nothing has to cross between parts.
All inputs are finite; a program needn't handle non-finite values.
Results may differ from a plain program's by a relative error of at most 0.00029.
Values sent between devices are 32-bit elements; how exact they have to be, the bound alone decides.
A program may use at most 128 MiB of HBM per device.

v0:
```python
import math

import jax
import jax.numpy as jnp
from jax import lax
from jax.sharding import PartitionSpec as P

STEPS = 3
CYCLES = 2


TIME_STEP = 0.01
INJECT_RATE = 1.0
INFLATION = 2.0
NOISE_CENTER = 127.5
NOISE_SPREAD = 73.9


def harmonic(first, second):
    return 2.0 * first * second / (first + second)


def plume_steps(perm_log, start_height, top_surface, porosity, well_mask):
    conduct = jnp.exp(perm_log)
    trans_rows = harmonic(conduct[:, :-1, :], conduct[:, 1:, :])
    trans_cols = harmonic(conduct[:, :, :-1], conduct[:, :, 1:])
    source = INJECT_RATE * well_mask.astype(jnp.float32)
    factor = TIME_STEP / porosity
    height = jnp.broadcast_to(start_height, perm_log.shape)
    for step_index in range(STEPS):
        level = height + top_surface
        flux_rows = (
            trans_rows
            * 0.5
            * (height[:, :-1, :] + height[:, 1:, :])
            * (level[:, :-1, :] - level[:, 1:, :])
        )
        flux_cols = (
            trans_cols
            * 0.5
            * (height[:, :, :-1] + height[:, :, 1:])
            * (level[:, :, :-1] - level[:, :, 1:])
        )
        inflow = jnp.pad(flux_rows, ((0, 0), (1, 0), (0, 0))) - jnp.pad(
            flux_rows, ((0, 0), (0, 1), (0, 0))
        )
        inflow = (
            inflow
            + jnp.pad(flux_cols, ((0, 0), (0, 0), (1, 0)))
            - jnp.pad(flux_cols, ((0, 0), (0, 0), (0, 1)))
        )
        height = height + factor * (inflow + source)
    return height


def make_innovation(predicted, observed, obs_error, noise):
    perturb = (noise.astype(jnp.float32) - NOISE_CENTER) / NOISE_SPREAD
    return (observed + math.sqrt(INFLATION) * obs_error * perturb - predicted) / obs_error


def gram_terms(predicted, innovation, obs_error):
    members = predicted.shape[0]
    scaled = (predicted - jnp.mean(predicted, axis=0, keepdims=True)) / (
        obs_error * math.sqrt(members - 1.0)
    )
    dims = (((1,), (1,)), ((), ()))
    gram = lax.dot_general(scaled, scaled, dims, precision=lax.Precision.HIGHEST)
    cross = lax.dot_general(scaled, innovation, dims, precision=lax.Precision.HIGHEST)
    return (gram, cross)


def solve_weights(gram, cross):
    members = gram.shape[0]
    full = gram + INFLATION * jnp.eye(members, dtype=jnp.float32)
    factor = jnp.linalg.cholesky(full)
    return jax.scipy.linalg.cho_solve((factor, True), cross)


def mix_fields(fields, weights):
    members = fields.shape[0]
    anomaly = (fields - jnp.mean(fields, axis=0, keepdims=True)) / math.sqrt(members - 1.0)
    return fields + lax.dot_general(
        weights, anomaly, (((0,), (0,)), ((), ())), precision=lax.Precision.HIGHEST
    )


def ensemble_solve(predicted, innovation, obs_error):
    whole_pred, whole_innov = (
        lax.all_gather(predicted, "member", axis=0, tiled=True),
        lax.all_gather(innovation, "member", axis=0, tiled=True),
    )
    gram, cross = gram_terms(whole_pred, whole_innov, obs_error)
    return solve_weights(gram, cross)


def on_device(
    perm_prior,
    start_height,
    top_surface,
    porosity,
    well_mask,
    obs_cells,
    observed,
    obs_error,
    noise_table,
):
    held_count, map_rows, map_cols = perm_prior.shape
    perm = perm_prior
    for cycle_index in range(CYCLES):
        height = plume_steps(perm, start_height, top_surface, porosity, well_mask)
        change = (height - start_height).reshape(held_count, map_rows * map_cols)
        predicted = jnp.take(change, obs_cells[cycle_index], axis=1)
        innovation = make_innovation(
            predicted, observed[cycle_index], obs_error, noise_table[cycle_index]
        )
        weights = ensemble_solve(predicted, innovation, obs_error)
        cell_major = lax.all_to_all(
            perm.reshape(held_count, map_rows * map_cols),
            "member",
            split_axis=1,
            concat_axis=0,
            tiled=True,
        )
        cell_major = mix_fields(cell_major, weights)
        returned = lax.all_to_all(cell_major, "member", split_axis=0, concat_axis=1, tiled=True)
        perm = returned.reshape(held_count, map_rows, map_cols)
    return perm


def solution(mesh):
    return jax.shard_map(
        on_device,
        mesh=mesh,
        in_specs=(
            P(("region", "member"), None, None),
            P("region", None),
            P("region", None),
            P("region", None),
            P("region", None),
            P("region", None),
            P("region", None),
            P("region"),
            P("region", "member", None),
        ),
        out_specs=P(("region", "member"), None, None),
        check_vma=False,
    )
```

profile of v0, /device:TPU:9, one launch (start us, length us, event | category | flops | bytes accessed | tf_op | source)
XLA Modules:
  0.0 204.6 jit_solution(7576748533026599066)
XLA Ops:
  0.0 1.3 all_to_all.50
  1.3 1.1 copy.81
  2.5 6.6 %all-to-all-start = ((f32[4,16,2048]{2,0,1:T(4,128)}), f32[4,16,2048]{2,0,1:T(4,128)S(1)}, u32[]{:S(2)}, u32[]{:S(2)}) async-start(f32[4,16,2048]{2,0,1:T(4,128)} %copy.81), calls=%async_computation | async-start | bytes 1048576 | tf_op jit(solution)/shard_map/all_to_all | solution.py:117
  9.0 1.1 exp.9
  11.2 1.1 slice_subtract_fusion.8
  12.3 1.0 slice_subtract_fusion.9
  15.5 1.2 broadcast_add_fusion.3
  18.9 8.7 %copy.82 = f32[4,64,512]{0,2,1:T(8,128)} copy(f32[4,64,512]{2,1,0:T(8,128)S(1)} %add_subtract_fusion.1) | data formatting | bytes 1048576 | tf_op jit(solution)/shard_map/sub | solution.py:111
  27.6 6.4 %gather_fusion = f32[128,4]{1,0:T(8,128)S(1)} fusion(f32[4,32768]{0,1:T(8,128)} %bitcast.88, s32[1024]{0:T(1024)S(1)} %pad_clamp_fusion.1), kind=kCustom, calls=%fused_computation.clone | custom fusion | bytes 4608 | tf_op jit(solution)/shard_map/jit(_take)/gather | solution.py:112
  34.2 18.8 %all-gather = f32[16,4,128]{2,1,0:T(4,128)S(1)} all-gather(f32[1,4,128]{2,1,0:T(4,128)S(1)} %copy.83), channel_id=1, replica_groups=mesh['region'=2,'member'=16] {'member'}, dimensions={0}, use_global_device_ids=true | all-gather | bytes 34816 | tf_op jit(solution)/shard_map/all_gather | solution.py:89
  53.4 5.8 %cholesky.44 = f32[64,64]{1,0:T(8,128)S(1)} custom-call(f32[64,64]{1,0:T(8,128)S(1)} %fusion.43), custom_call_target="Cholesky" | custom-call | tf_op jit(solution)/shard_map/jit(cholesky)/cholesky | solution.py:75
  60.7 4.9 %custom-call.8 = f32[1,64,64]{1,2,0:T(8,128)S(1)} custom-call(f32[1,64,64]{2,1,0:T(8,128)S(1)} %fusion.32), custom_call_target="InvertDiagBlocksLowerTriangular" | custom-call | tf_op jit(solution)/shard_map/jit(_cho_solve)/triangular_solve | solution.py:76
  66.0 17.5 %all-gather.1 = f32[16,4,128]{2,1,0:T(4,128)S(1)} all-gather(f32[1,4,128]{2,1,0:T(4,128)S(1)} %copy.87), channel_id=1, replica_groups=mesh['region'=2,'member'=16] {'member'}, dimensions={0}, use_global_device_ids=true | all-gather | bytes 34816 | tf_op jit(solution)/shard_map/all_gather | solution.py:90
  86.0 6.5 %all-to-all-start.1 = ((f32[16,4,2048]{2,1,0:T(4,128)}), f32[16,4,2048]{2,1,0:T(4,128)S(1)}, u32[]{:S(2)}, u32[]{:S(2)}) async-start(f32[16,4,2048]{2,1,0:T(4,128)} %all_to_all.54), calls=%async_computation.1 | async-start | bytes 1048576 | tf_op jit(solution)/shard_map/all_to_all | solution.py:125
  92.5 14.1 %all-to-all-done.1 = f32[16,4,2048]{2,1,0:T(4,128)S(1)} async-done(((f32[16,4,2048]{2,1,0:T(4,128)}), f32[16,4,2048]{2,1,0:T(4,128)S(1)}, u32[]{:S(2)}, u32[]{:S(2)}) %all-to-all-start.1) | async-done | bytes 524320 | tf_op jit(solution)/shard_map/all_to_all | solution.py:125
  109.9 8.7 %copy.90 = f32[4,64,512]{0,2,1:T(8,128)} copy(f32[4,64,512]{2,1,0:T(8,128)S(1)} %add_subtract_fusion) | data formatting | bytes 1048576 | tf_op jit(solution)/shard_map/sub | solution.py:111
  118.6 6.4 %gather_fusion.1 = f32[128,4]{1,0:T(8,128)S(1)} fusion(f32[4,32768]{0,1:T(8,128)} %bitcast.89, s32[1024]{0:T(1024)S(1)} %pad_clamp_fusion), kind=kCustom, calls=%fused_computation.1.clone | custom fusion | bytes 4608 | tf_op jit(solution)/shard_map/jit(_take)/gather | solution.py:112
  125.1 17.2 %all-gather.2 = f32[16,4,128]{2,1,0:T(4,128)S(1)} all-gather(f32[1,4,128]{2,1,0:T(4,128)S(1)} %copy.91), channel_id=1, replica_groups=mesh['region'=2,'member'=16] {'member'}, dimensions={0}, use_global_device_ids=true | all-gather | bytes 34816 | tf_op jit(solution)/shard_map/all_gather | solution.py:89
  142.6 5.8 %cholesky.55 = f32[64,64]{1,0:T(8,128)S(1)} custom-call(f32[64,64]{1,0:T(8,128)S(1)} %fusion.38), custom_call_target="Cholesky" | custom-call | tf_op jit(solution)/shard_map/jit(cholesky)/cholesky | solution.py:75
  149.6 1.1 copy.89
  150.7 6.5 %all-to-all-start.2 = ((f32[4,16,2048]{2,0,1:T(4,128)}), f32[4,16,2048]{2,0,1:T(4,128)S(1)}, u32[]{:S(2)}, u32[]{:S(2)}) async-start(f32[4,16,2048]{2,0,1:T(4,128)} %copy.89), calls=%async_computation.2 | async-start | bytes 1048576 | tf_op jit(solution)/shard_map/all_to_all | solution.py:117
  157.9 4.9 %custom-call.9 = f32[1,64,64]{1,2,0:T(8,128)S(1)} custom-call(f32[1,64,64]{2,1,0:T(8,128)S(1)} %fusion.33), custom_call_target="InvertDiagBlocksLowerTriangular" | custom-call | tf_op jit(solution)/shard_map/jit(_cho_solve)/triangular_solve | solution.py:76
  163.0 19.0 %all-gather.3 = f32[16,4,128]{2,1,0:T(4,128)S(1)} all-gather(f32[1,4,128]{2,1,0:T(4,128)S(1)} %copy.95), channel_id=1, replica_groups=mesh['region'=2,'member'=16] {'member'}, dimensions={0}, use_global_device_ids=true | all-gather | bytes 34816 | tf_op jit(solution)/shard_map/all_gather | solution.py:90
  183.7 19.7 %all_to_all.67 = f32[16,4,2048]{2,1,0:T(4,128)S(1)} all-to-all(f32[16,4,2048]{2,1,0:T(4,128)S(1)} %all_to_all.60), channel_id=1, replica_groups=mesh['region'=2,'member'=16] {'member'}, dimensions={0} | all-to-all | bytes 1048576 | tf_op jit(solution)/shard_map/all_to_all | solution.py:125
  (87 shorter events, 18.7 us)
Async XLA Ops:
  0.0 18.6 %copy-start = (f32[64,512]{1,0:T(8,128)S(1)}, f32[64,512]{1,0:T(8,128)}, u32[]{:S(2)}) copy-start(f32[64,512]{1,0:T(8,128)} %param.15) | copy-start | bytes 393220
  0.0 17.6 %copy-start.1 = (f32[64,512]{1,0:T(8,128)S(1)}, f32[64,512]{1,0:T(8,128)}, u32[]{:S(2)}) copy-start(f32[64,512]{1,0:T(8,128)} %param.16) | copy-start | bytes 393220
  2.5 81.6 %all-to-all-start = ((f32[4,16,2048]{2,0,1:T(4,128)}), f32[4,16,2048]{2,0,1:T(4,128)S(1)}, u32[]{:S(2)}, u32[]{:S(2)}) async-start(f32[4,16,2048]{2,0,1:T(4,128)} %copy.81), calls=%async_computation | async-start | bytes 1048576 | tf_op jit(solution)/shard_map/all_to_all | solution.py:117
  17.1 10.6 %copy-start.4 = (s32[2,128]{1,0:T(2,128)S(1)}, s32[2,128]{1,0:T(2,128)}, u32[]{:S(2)}) copy-start(s32[2,128]{1,0:T(2,128)} %param.19) | copy-start | bytes 3076
  17.1 36.0 %copy-start.3 = (f32[128]{0:T(128)S(1)}, f32[128]{0:T(128)}, u32[]{:S(2)}) copy-start(f32[128]{0:T(128)} %param.21) | copy-start | bytes 1540
  17.1 43.6 %copy-start.2 = (s32[2,4,128]{2,1,0:T(4,128)S(1)}, s32[2,4,128]{2,1,0:T(4,128)}, u32[]{:S(2)}) copy-start(s32[2,4,128]{2,1,0:T(4,128)} %param.22) | copy-start | bytes 12292
  17.1 43.6 %copy-start.5 = (f32[2,128]{1,0:T(2,128)S(1)}, f32[2,128]{1,0:T(2,128)}, u32[]{:S(2)}) copy-start(f32[2,128]{1,0:T(2,128)} %param.20) | copy-start | bytes 3076
  86.0 20.6 %all-to-all-start.1 = ((f32[16,4,2048]{2,1,0:T(4,128)}), f32[16,4,2048]{2,1,0:T(4,128)S(1)}, u32[]{:S(2)}, u32[]{:S(2)}) async-start(f32[16,4,2048]{2,1,0:T(4,128)} %all_to_all.54), calls=%async_computation.1 | async-start | bytes 1048576 | tf_op jit(solution)/shard_map/all_to_all | solution.py:125
  150.7 31.9 %all-to-all-start.2 = ((f32[4,16,2048]{2,0,1:T(4,128)}), f32[4,16,2048]{2,0,1:T(4,128)S(1)}, u32[]{:S(2)}, u32[]{:S(2)}) async-start(f32[4,16,2048]{2,0,1:T(4,128)} %copy.89), calls=%async_computation.2 | async-start | bytes 1048576 | tf_op jit(solution)/shard_map/all_to_all | solution.py:117
where the time goes:
time: 207 us; the launch traced here: 205 us
  blocking collectives  92.2 us (45%)
  local copies, waits for them, and re-layouts  39 us (19%)
  other arithmetic  36.6 us (18%)
  starting transfers between devices  19.5 us (9%)
  waiting for transfers between devices  14.1 us (7%)
  matrix products  2.8 us (1%)
    all_gather x2, blocking collectives, ensemble_solve(): lax.all_gather(innovation, 'member', axis=0, tiled=True)  36.5 us
    all_gather x2, blocking collectives, ensemble_solve(): lax.all_gather(predicted, 'member', axis=0, tiled=True)  36 us
    all_to_all x1, blocking collectives, on_device(): lax.all_to_all(cell_major, 'member', split_axis=0, concat_axis=1, tiled=T...  19.7 us
    sub x2, local copies, waits for them, and re-layouts, on_device(): change = (height - start_height).reshape(held_count, map_rows * map_cols)  17.3 us
    all_to_all x1, waiting for transfers between devices, on_device(): lax.all_to_all(cell_major, 'member', split_axis=0, concat_axis=1, tiled=T...  14.1 us
    another operation x6, other arithmetic, solve_weights(): factor = jnp.linalg.cholesky(full)  13.2 us
    all_to_all x2, starting transfers between devices, on_device(): lax.all_to_all(perm.reshape(held_count, map_rows * map_cols), 'member', s...  13 us
    gather x2, local copies, waits for them, and re-layouts, on_device(): predicted = jnp.take(change, obs_cells[cycle_index], axis=1)  12.8 us
  transfers between devices with their start and end apart: 3, of which 1 were waited for; matrix products, arithmetic and copies ran while one was open for 22% of the time, Pallas kernels for 0%

commit v1 on v0

--- a/solution.py
+++ b/solution.py
@@ -1,9 +1,20 @@
+import functools
 import math
 
 import jax
 import jax.numpy as jnp
 from jax import lax
+from jax.experimental import pallas as pl
+from jax.experimental.pallas import tpu as pltpu
 from jax.sharding import PartitionSpec as P
+
+MESH = pl.DeviceIdType.MESH
+HIGHEST = lax.Precision.HIGHEST
+SIDE = 8
+PATCH = SIDE * SIDE
+LANES = 128
+PAIR = LANES // PATCH
+FIELDS = 8
 
 STEPS = 3
 CYCLES = 2
@@ -127,9 +138,401 @@
     return perm
 
 
+def patch_plume(perm_log, start, top, porosity, well):
+    axis = perm_log.ndim - 1
+    lane = lax.broadcasted_iota(jnp.int32, perm_log.shape, axis)
+    inner_col = (lane % SIDE) < SIDE - 1
+    inner_row = (lane % PATCH) < PATCH - SIDE
+
+    def ahead(x, by):
+        return pltpu.roll(x, LANES - by, axis)
+
+    def behind(x, by):
+        return pltpu.roll(x, by, axis)
+
+    conduct = jnp.exp(perm_log)
+    half_cols = jnp.where(inner_col, 0.5 * harmonic(conduct, ahead(conduct, 1)), 0.0)
+    half_rows = jnp.where(inner_row, 0.5 * harmonic(conduct, ahead(conduct, SIDE)), 0.0)
+    source = INJECT_RATE * well
+    factor = TIME_STEP / porosity
+    begin = jnp.broadcast_to(start, perm_log.shape)
+    height = begin
+    for _ in range(STEPS):
+        level = height + top
+        flux_cols = half_cols * (height + ahead(height, 1)) * (level - ahead(level, 1))
+        flux_rows = half_rows * (height + ahead(height, SIDE)) * (level - ahead(level, SIDE))
+        inflow = behind(flux_cols, 1) - flux_cols + behind(flux_rows, SIDE) - flux_rows
+        height = height + factor * (inflow + source)
+    return height - begin
+
+
+def local_kernel(
+    cells_ref,
+    perm_ref,
+    start_ref,
+    top_ref,
+    porosity_ref,
+    well_ref,
+    observed_ref,
+    error_ref,
+    noise_ref,
+    first_ref,
+    patch_ref,
+    mark_ref,
+    stack,
+    patch_one,
+    mark_one,
+):
+    held, rows, cols = perm_ref.shape
+    nobs = observed_ref.shape[1]
+    for strip in range(cols // LANES):
+        across = slice(strip * LANES, (strip + 1) * LANES)
+        fields = [perm_ref[member, :, across] for member in range(held)]
+        fields += [start_ref[:, across], top_ref[:, across], porosity_ref[:, across]]
+        fields += [well_ref[:, across].astype(jnp.float32)]
+        for index, field in enumerate(fields):
+            stack[strip, pl.ds(index, rows, stride=FIELDS), :] = field
+
+    lane = lax.broadcasted_iota(jnp.int32, (FIELDS, LANES), 1)
+
+    for cycle in range(CYCLES):
+        patches, marks = (patch_one, mark_one) if cycle == 0 else (patch_ref, mark_ref)
+
+        @functools.partial(lax.fori_loop, 0, nobs // PAIR, init_val=0, unroll=4)
+        def _(chunk, carry):
+            total = jnp.zeros((FIELDS, LANES), jnp.float32)
+            mark = jnp.zeros((FIELDS, LANES), jnp.float32)
+            for part in range(PAIR):
+                cell = cells_ref[cycle, chunk * PAIR + part]
+                row, col = lax.div(cell, cols), lax.rem(cell, cols)
+                row0 = jnp.clip(row - STEPS, 0, rows - SIDE)
+                col0 = jnp.clip(col - STEPS, 0, cols - SIDE)
+                low = lax.div(col0, LANES)
+                high = jnp.minimum(low + 1, cols // LANES - 1)
+                within = col0 - low * LANES
+                for i in range(SIDE):
+                    at = pl.multiple_of((row0 + i) * FIELDS, FIELDS)
+                    left = stack[low, pl.ds(at, FIELDS), :]
+                    right = stack[high, pl.ds(at, FIELDS), :]
+                    window = jnp.where(lane >= within, left, right)
+                    place = part * PATCH + i * SIDE
+                    moved = pltpu.roll(window, lax.rem(place + LANES - within, LANES), 1)
+                    total = jnp.where((lane >= place) & (lane < place + SIDE), moved, total)
+                spot = part * PATCH + (row - row0) * SIDE + (col - col0)
+                mark = jnp.where(lane == spot, 1.0, mark)
+            patches[chunk] = total
+            marks[chunk] = mark
+            return carry
+
+    group = 8
+    wide = lax.broadcasted_iota(jnp.int32, (group, held, LANES), 2)
+    turn = lax.broadcasted_iota(jnp.int32, (group, held, LANES), 0)
+
+    def run(index, acc):
+        at = pl.ds(index * group, group)
+        change = patch_plume(
+            patch_one[at, 0:held, :],
+            patch_one[at, held : held + 1, :],
+            patch_one[at, held + 1 : held + 2, :],
+            patch_one[at, held + 2 : held + 3, :],
+            patch_one[at, held + 3 : held + 4, :],
+        )
+        change = change * mark_one[at, 0:held, :]
+        for part in range(PAIR):
+            here = (wide >= part * PATCH) & (wide < (part + 1) * PATCH)
+            sums = jnp.sum(jnp.where(here, change, 0.0), axis=2, keepdims=True)
+            slot = (index * group + turn) * PAIR + part
+            acc = acc + jnp.sum(jnp.where(wide == slot, sums, 0.0), axis=0)
+        return acc
+
+    predicted = lax.fori_loop(
+        0, nobs // (PAIR * group), run, jnp.zeros((held, nobs), jnp.float32)
+    )
+    error = error_ref[...]
+    first_ref[0:held, :] = predicted
+    first_ref[held : 2 * held, :] = make_innovation(
+        predicted, observed_ref[0:1, :], error, noise_ref[0]
+    )
+    first_ref[2 * held : 3 * held, :] = make_innovation(
+        jnp.zeros_like(predicted), observed_ref[1:2, :], error, noise_ref[1]
+    )
+    first_ref[3 * held : 4 * held, :] = jnp.zeros_like(predicted)
+
+
+def dot(a, b, dims):
+    return lax.dot_general(
+        a, b, (dims, ((), ())), precision=HIGHEST, preferred_element_type=jnp.float32
+    )
+
+
+def eliminate(gram, cross):
+    size = gram.shape[0]
+    work = jnp.concatenate([gram, cross], axis=1)
+    line = lax.broadcasted_iota(jnp.int32, work.shape, 0)
+    for k in range(size):
+        row = work[k : k + 1, :] * (1.0 / work[k : k + 1, k : k + 1])
+        work = jnp.where(line == k, row, work - work[:, k : k + 1] * row)
+    return work[:, size:]
+
+
+def add_inflation(gram):
+    one = lax.broadcasted_iota(jnp.int32, gram.shape, 0)
+    two = lax.broadcasted_iota(jnp.int32, gram.shape, 1)
+    return jnp.where(one == two, gram + INFLATION, gram)
+
+
+def mix(fields, weights):
+    members = fields.shape[0]
+    anomaly = (fields - jnp.mean(fields, axis=0, keepdims=True)) / math.sqrt(members - 1.0)
+    return fields + dot(weights, anomaly, ((0,), (0,)))
+
+
+def ensemble_kernel(
+    count,
+    perm_ref,
+    first_ref,
+    patch_ref,
+    mark_ref,
+    error_ref,
+    error_col_ref,
+    out_ref,
+    first_all,
+    patch_all,
+    pred_all,
+    block,
+    mixed,
+    send_sem,
+    recv_sem,
+    local_sem,
+):
+    held, rows, cols = perm_ref.shape
+    members = held * count
+    nobs = error_ref.shape[1]
+    own_obs = nobs // count
+    own_chunks = own_obs // PAIR
+    me = lax.axis_index("member")
+    _, tall, wide = block.shape
+    across = cols // wide
+
+    def cells_of(ref, device):
+        return ref.at[
+            :,
+            pl.ds(pl.multiple_of((device // across) * tall, tall), tall),
+            pl.ds(pl.multiple_of((device % across) * wide, wide), wide),
+        ]
+
+    def members_of(ref, device):
+        return ref.at[pl.ds(device * held, held)]
+
+    def obs_of(ref, device):
+        return ref.at[pl.ds(pl.multiple_of(device * own_obs, own_obs), own_obs)]
+
+    def chunks_of(ref, device):
+        return ref.at[pl.ds(device * own_chunks, own_chunks)]
+
+    ways = [
+        (lambda peer: first_ref, lambda owner: first_all.at[owner]),
+        (lambda peer: chunks_of(patch_ref, peer), lambda owner: patch_all.at[owner]),
+        (lambda peer: cells_of(perm_ref, peer), lambda owner: members_of(block, owner)),
+        (lambda peer: obs_of(pred_all, me), lambda owner: obs_of(pred_all, owner)),
+        (lambda peer: members_of(mixed, peer), lambda owner: cells_of(out_ref, owner)),
+    ]
+
+    def transfer(kind, peer, owner, slot):
+        source, target = ways[kind]
+        return pltpu.make_async_remote_copy(
+            src_ref=source(peer),
+            dst_ref=target(owner),
+            send_sem=send_sem.at[kind, slot],
+            recv_sem=recv_sem.at[kind, slot],
+            device_id={"member": peer},
+            device_id_type=MESH,
+        )
+
+    def each(body):
+        def step(j, carry):
+            body(j)
+            return carry
+
+        lax.fori_loop(1, count, step, 0)
+
+    def send(kind):
+        each(lambda j: transfer(kind, lax.rem(me + j, count), me, j).start())
+
+    def receive(kind):
+        each(lambda j: transfer(kind, me, lax.rem(me + count - j, count), j).wait_recv())
+
+    def sent(kind):
+        each(lambda j: transfer(kind, lax.rem(me + j, count), me, j).wait_send())
+
+    barrier = pltpu.get_barrier_semaphore()
+    each(
+        lambda j: pl.semaphore_signal(
+            barrier,
+            inc=1,
+            device_id={"member": lax.rem(me + j, count)},
+            device_id_type=MESH,
+        )
+    )
+    pl.semaphore_wait(barrier, count - 1)
+
+    send(0)
+    send(1)
+    send(2)
+    own_in = pltpu.make_async_copy(cells_of(perm_ref, me), members_of(block, me), local_sem.at[0])
+    own_in.start()
+    first_all[me] = first_ref[...]
+    patch_all[me] = patch_ref[pl.ds(me * own_chunks, own_chunks)]
+
+    depth = first_ref.shape[0]
+    line = lax.broadcasted_iota(jnp.int32, (members, count * depth), 0)
+    spot = lax.broadcasted_iota(jnp.int32, (members, count * depth), 1)
+    home = (line // held) * depth + line % held
+
+    def pick(whole, offset):
+        return dot(jnp.where(spot == home + offset, 1.0, 0.0), whole, ((1,), (0,)))
+
+    error = error_ref[...]
+    root = math.sqrt(members - 1.0)
+
+    receive(0)
+    whole = first_all[...].reshape(count * depth, nobs)
+    predicted = pick(whole, 0)
+    innovation = pick(whole, held)
+    base = pick(whole, 2 * held)
+    scaled = (predicted - jnp.mean(predicted, axis=0, keepdims=True)) / (error * root)
+    both = dot(scaled, jnp.concatenate([scaled, innovation], axis=0), ((1,), (1,)))
+    first_weights = eliminate(add_inflation(both[:, :members]), both[:, members:])
+
+    receive(1)
+    line2 = lax.broadcasted_iota(jnp.int32, (members, count * FIELDS), 0)
+    spot2 = lax.broadcasted_iota(jnp.int32, (members, count * FIELDS), 1)
+    choose = jnp.where(spot2 == (line2 // held) * FIELDS + line2 % held, 1.0, 0.0)
+    fresh = jnp.zeros((own_obs, members), jnp.float32)
+    one = lax.broadcasted_iota(jnp.int32, (own_obs, LANES), 0)
+    two = lax.broadcasted_iota(jnp.int32, (own_obs, LANES), 1)
+    for q in range(own_chunks):
+        at = me * own_chunks + q
+        values = patch_all[:, q].reshape(count * FIELDS, LANES)
+        prior = dot(choose, values, ((1,), (0,)))
+        change = patch_plume(
+            mix(prior, first_weights),
+            patch_ref[at, held : held + 1, :],
+            patch_ref[at, held + 1 : held + 2, :],
+            patch_ref[at, held + 2 : held + 3, :],
+            patch_ref[at, held + 3 : held + 4, :],
+        )
+        change = change * mark_ref[at, 0:1, :]
+        ones = jnp.where(two // PATCH + q * PAIR == one, 1.0, 0.0)
+        fresh = fresh + dot(ones, change, ((1,), (1,)))
+    pred_all[pl.ds(pl.multiple_of(me * own_obs, own_obs), own_obs), 0:members] = fresh
+    pred_all[pl.ds(pl.multiple_of(me * own_obs, own_obs), own_obs), members:] = jnp.zeros(
+        (own_obs, pred_all.shape[1] - members), jnp.float32
+    )
+    send(3)
+
+    receive(2)
+    own_in.wait()
+    for r in range(tall):
+        mixed[:, r, :] = mix(block[:, r, :], first_weights)
+
+    receive(3)
+    table = pred_all[:, 0:members]
+    error_col = error_col_ref[:, 0:1]
+    scaled2 = (table - jnp.mean(table, axis=1, keepdims=True)) / (error_col * root)
+    gram = dot(scaled2, scaled2, ((0,), (0,)))
+    cross = dot(scaled2, base, ((0,), (1,))) - dot(scaled2, table / error_col, ((0,), (0,)))
+    second_weights = eliminate(add_inflation(gram), cross)
+    for r in range(tall):
+        mixed[:, r, :] = mix(mixed[:, r, :], second_weights)
+    send(4)
+    own_out = pltpu.make_async_copy(members_of(mixed, me), cells_of(out_ref, me), local_sem.at[1])
+    own_out.start()
+    for kind in range(4):
+        sent(kind)
+    own_out.wait()
+    receive(4)
+    sent(4)
+
+
+def patch_device(count, perm, start, top, porosity, well, cells, observed, error, noise):
+    held, rows, cols = perm.shape
+    nobs = observed.shape[1]
+    members = held * count
+    chunks = nobs // PAIR
+    vmem = pl.BlockSpec(memory_space=pltpu.VMEM)
+    first, patch, mark = pl.pallas_call(
+        local_kernel,
+        out_shape=[
+            jax.ShapeDtypeStruct((4 * held, nobs), jnp.float32),
+            jax.ShapeDtypeStruct((chunks, FIELDS, LANES), jnp.float32),
+            jax.ShapeDtypeStruct((chunks, FIELDS, LANES), jnp.float32),
+        ],
+        in_specs=[pl.BlockSpec(memory_space=pltpu.SMEM)] + [vmem] * 8,
+        out_specs=[vmem] * 3,
+        scratch_shapes=[
+            pltpu.VMEM((cols // LANES, rows * FIELDS, LANES), jnp.float32),
+            pltpu.VMEM((chunks, FIELDS, LANES), jnp.float32),
+            pltpu.VMEM((chunks, FIELDS, LANES), jnp.float32),
+        ],
+        compiler_params=pltpu.CompilerParams(vmem_limit_bytes=32 * 1024 * 1024),
+    )(cells, perm, start, top, porosity, well, observed, error.reshape(1, nobs), noise)
+    across = (count * SIDE) // rows
+    wide = cols // across
+    kinds = 5
+    return pl.pallas_call(
+        functools.partial(ensemble_kernel, count),
+        out_shape=jax.ShapeDtypeStruct(perm.shape, jnp.float32),
+        in_specs=[vmem] * 6,
+        out_specs=vmem,
+        scratch_shapes=[
+            pltpu.VMEM((count, 4 * held, nobs), jnp.float32),
+            pltpu.VMEM((count, chunks // count, FIELDS, LANES), jnp.float32),
+            pltpu.VMEM((nobs, LANES), jnp.float32),
+            pltpu.VMEM((members, SIDE, wide), jnp.float32),
+            pltpu.VMEM((members, SIDE, wide), jnp.float32),
+            pltpu.SemaphoreType.DMA((kinds, count)),
+            pltpu.SemaphoreType.DMA((kinds, count)),
+            pltpu.SemaphoreType.DMA((2,)),
+        ],
+        compiler_params=pltpu.CompilerParams(
+            collective_id=0, has_side_effects=True, vmem_limit_bytes=32 * 1024 * 1024
+        ),
+    )(
+        perm,
+        first,
+        patch,
+        mark,
+        error.reshape(1, nobs),
+        jnp.broadcast_to(error.reshape(nobs, 1), (nobs, LANES)),
+    )
+
+
+def fits(count, held, rows, cols, nobs):
+    members, own_obs = count * held, nobs // count
+    return (
+        held == FIELDS // 2
+        and members <= LANES // 2
+        and nobs == LANES
+        and nobs == own_obs * count
+        and own_obs % 8 == 0
+        and rows % SIDE == 0
+        and (count * SIDE) % rows == 0
+        and cols % ((count * SIDE // rows) * LANES) == 0
+    )
+
+
+def device_program(perm, *rest):
+    count = lax.axis_size("member")
+    held, rows, cols = perm.shape
+    if fits(count, held, rows, cols, rest[5].shape[1]):
+        return patch_device(count, perm, *rest)
+    return on_device(perm, *rest)
+
+
 def solution(mesh):
     return jax.shard_map(
-        on_device,
+        device_program,
         mesh=mesh,
         in_specs=(
             P(("region", "member"), None, None),

time: 207 us -> 70.2 us (0.34); the launches traced: 205 us -> 70 us
  blocking collectives: 92.2 us -> 0 us
  Pallas kernels: 0 us -> 63.1 us
  other arithmetic: 36.6 us -> 0 us
  local copies, waits for them, and re-layouts: 39 us -> 6.82 us
  starting transfers between devices: 19.5 us -> 0 us
  waiting for transfers between devices: 14.1 us -> 0 us
  matrix products: 2.8 us -> 0 us
    all_gather x4 -> x0, blocking collectives: 72.5 us -> none  [the longest x2 36.5 us: ensemble_solve(): lax.all_gather(innovation, 'member', axis=0, tiled=True)]
    pallas_call x0 -> x2, Pallas kernels: none -> 63.1 us  [the longest x1 48.2 us: patch_device(): pl.pallas_call(functools.partial(ensemble_kernel, count), out_shape=jax.S...]
    another operation x10 -> x0, other arithmetic: 24.4 us -> none  [the longest x6 13.2 us: solve_weights(): factor = jnp.linalg.cholesky(full)]
    all_to_all x1 -> x0, blocking collectives: 19.7 us -> none  [on_device(): lax.all_to_all(cell_major, 'member', split_axis=0, concat_axis=1, tiled=T...]
    all_to_all x3 -> x0, starting transfers between devices: 19.5 us -> none  [the longest x2 13 us: on_device(): lax.all_to_all(perm.reshape(held_count, map_rows * map_cols), 'member', s...]
    sub x2 -> x0, local copies, waits for them, and re-layouts: 17.3 us -> none  [on_device(): change = (height - start_height).reshape(held_count, map_rows * map_cols)]
    all_to_all x3 -> x0, waiting for transfers between devices: 14.1 us -> none  [the longest x1 14.1 us: on_device(): lax.all_to_all(cell_major, 'member', split_axis=0, concat_axis=1, tiled=T...]
    gather x2 -> x0, local copies, waits for them, and re-layouts: 12.8 us -> none  [on_device(): predicted = jnp.take(change, obs_cells[cycle_index], axis=1)]
  transfers between devices with their start and end apart: 3 -> 0, of which waited for: 1 -> 0; matrix products, arithmetic and copies ran while one was open for 22% -> 0% of each run, Pallas kernels for 0% -> 0%
where the time goes in v1:
time: 70.2 us; the launch traced here: 70 us
  Pallas kernels  63.1 us (90%)
  local copies, waits for them, and re-layouts  6.82 us (10%)
    pallas_call x1, Pallas kernels, patch_device(): pl.pallas_call(functools.partial(ensemble_kernel, count), out_shape=jax.S...  48.2 us
    pallas_call x1, Pallas kernels, patch_device(): pl.pallas_call(local_kernel, out_shape=[jax.ShapeDtypeStruct((4 * held, n...  14.9 us
    unnamed x21, local copies, waits for them, and re-layouts  6.74 us

profile of v1, /device:TPU:9, one launch (start us, length us, event | category | flops | bytes accessed | tf_op | source)
XLA Modules:
  0.0 70.0 jit_solution(1329797641924817711)
XLA Ops:
  0.0 0.0 copy-start.6
  0.0 0.7 copy-done.6
  0.7 0.0 copy-start.7
  0.7 0.0 copy-start.8
  0.7 0.0 copy-start.9
  0.7 0.1 broadcast_in_dim.2.error_col_ref
  0.7 0.6 copy-done.7
  1.3 0.0 copy-done.8
  1.4 0.0 copy-done.9
  1.4 0.0 copy-start
  1.4 1.0 %copy-done = f32[4,64,512]{2,1,0:T(8,128)S(1)} copy-done((f32[4,64,512]{2,1,0:T(8,128)S(1)}, f32[4,64,512]{2,1,0:T(8,128)}, u32[]{:S(2)}) %copy-start) | copy-done | bytes 524312
  2.4 0.0 copy-start.2
  2.4 0.9 %copy-done.2 = f32[64,512]{1,0:T(8,128)S(1)} copy-done((f32[64,512]{1,0:T(8,128)S(1)}, f32[64,512]{1,0:T(8,128)}, u32[]{:S(2)}) %copy-start.2) | copy-done | bytes 131096
  3.3 0.0 copy-start.3
  3.3 0.9 %copy-done.3 = f32[64,512]{1,0:T(8,128)S(1)} copy-done((f32[64,512]{1,0:T(8,128)S(1)}, f32[64,512]{1,0:T(8,128)}, u32[]{:S(2)}) %copy-start.3) | copy-done | bytes 131096
  4.2 0.0 copy-start.4
  4.2 0.9 %copy-done.4 = f32[64,512]{1,0:T(8,128)S(1)} copy-done((f32[64,512]{1,0:T(8,128)S(1)}, f32[64,512]{1,0:T(8,128)}, u32[]{:S(2)}) %copy-start.4) | copy-done | bytes 131096
  5.1 0.0 copy-start.5
  5.1 0.9 %copy-done.5 = s32[64,512]{1,0:T(8,128)S(1)} copy-done((s32[64,512]{1,0:T(8,128)S(1)}, s32[64,512]{1,0:T(8,128)}, u32[]{:S(2)}) %copy-start.5) | copy-done | bytes 131096
  6.0 0.0 copy-start.1
  6.0 14.9 %shard_map.91 = (f32[16,128]{1,0:T(8,128)S(1)}, f32[64,8,128]{2,1,0:T(8,128)S(1)}, f32[64,8,128]{2,1,0:T(8,128)S(1)}) custom-call(s32[2,128]{1,0:T(2,128)S(1)} %copy-done.8, f32[4,64,512]{2,1,0:T(8,128)S(1)} %copy-done, f32[64,512]{1,0:T(8,128)S(1)} %copy-done.2, f32[64,512]{1,0:T(8,128)S(1)} %copy-done.3, f32[64,512]{1,0:T(8,128)S(1)} %copy-done.4, ...), custom_call_target="tpu_custom_call" | custom-call | tf_op jit(solution)/shard_map/pallas_call | solution.py:464
  20.9 0.0 copy-done.1
  20.9 48.2 %shard_map.92 = f32[4,64,512]{2,1,0:T(8,128)S(1)} custom-call(f32[4,64,512]{2,1,0:T(8,128)S(1)} %copy-done.1, f32[16,128]{1,0:T(8,128)S(1)} %get-tuple-element.8.first_ref, f32[64,8,128]{2,1,0:T(8,128)S(1)} %get-tuple-element.9.patch_ref, f32[64,8,128]{2,1,0:T(8,128)S(1)} %get-tuple-element.10.mark_ref, f32[1,128]{1,0:T(1,128)S(1)} %bitcast.2, ...), custom_call_target="tpu_custom_call" | custom-call | tf_op jit(solution)/shard_map/pallas_call | solution.py:483
  69.2 0.8 %copy.11 = f32[4,64,512]{2,1,0:T(8,128)} copy(f32[4,64,512]{2,1,0:T(8,128)S(1)} %shard_map.92) | data formatting | bytes 1048576
Async XLA Ops:
  0.0 0.7 copy-start.6
  0.7 0.7 copy-start.7
  0.7 0.7 copy-start.8
  0.7 0.7 %copy-start.9 = (f32[2,128]{1,0:T(2,128)S(1)}, f32[2,128]{1,0:T(2,128)}, u32[]{:S(2)}) copy-start(f32[2,128]{1,0:T(2,128)} %observed_ref.1) | copy-start | bytes 3076
  1.4 1.0 %copy-start = (f32[4,64,512]{2,1,0:T(8,128)S(1)}, f32[4,64,512]{2,1,0:T(8,128)}, u32[]{:S(2)}) copy-start(f32[4,64,512]{2,1,0:T(8,128)} %perm_ref.3) | copy-start | bytes 1572868
  2.4 0.9 %copy-start.2 = (f32[64,512]{1,0:T(8,128)S(1)}, f32[64,512]{1,0:T(8,128)}, u32[]{:S(2)}) copy-start(f32[64,512]{1,0:T(8,128)} %start_ref.1) | copy-start | bytes 393220
  3.3 0.9 %copy-start.3 = (f32[64,512]{1,0:T(8,128)S(1)}, f32[64,512]{1,0:T(8,128)}, u32[]{:S(2)}) copy-start(f32[64,512]{1,0:T(8,128)} %top_ref.1) | copy-start | bytes 393220
  4.2 0.9 %copy-start.4 = (f32[64,512]{1,0:T(8,128)S(1)}, f32[64,512]{1,0:T(8,128)}, u32[]{:S(2)}) copy-start(f32[64,512]{1,0:T(8,128)} %porosity_ref.1) | copy-start | bytes 393220
  5.1 0.9 %copy-start.5 = (s32[64,512]{1,0:T(8,128)S(1)}, s32[64,512]{1,0:T(8,128)}, u32[]{:S(2)}) copy-start(s32[64,512]{1,0:T(8,128)} %well_ref.1) | copy-start | bytes 393220
  6.0 14.9 %copy-start.1 = (f32[4,64,512]{2,1,0:T(8,128)S(1)}, f32[4,64,512]{2,1,0:T(8,128)}, u32[]{:S(2)}) copy-start(f32[4,64,512]{2,1,0:T(8,128)} %perm_ref.3) | copy-start | bytes 1572868

commit v2 on v0

--- a/solution.py
+++ b/solution.py
@@ -1,9 +1,22 @@
+import functools
 import math
 
 import jax
 import jax.numpy as jnp
 from jax import lax
+from jax.experimental import pallas as pl
+from jax.experimental.pallas import tpu as pltpu
 from jax.sharding import PartitionSpec as P
+
+MESH = pl.DeviceIdType.MESH
+HIGHEST = lax.Precision.HIGHEST
+SIDE = 8
+LANES = 128
+HALF = LANES // 2
+QUARTERS = SIDE // 2
+FIELDS = 8
+SUBLANES = 8
+KINDS = 5
 
 STEPS = 3
 CYCLES = 2
@@ -127,9 +140,492 @@
     return perm
 
 
+def patch_plume(perm_log, start, top, porosity, well):
+    axis = perm_log[0].ndim - 1
+    lane = lax.broadcasted_iota(jnp.int32, perm_log[0].shape, axis)
+    inner_col = (lane % SIDE) < SIDE - 1
+    upper = lane < HALF
+
+    def right_of(x):
+        return pltpu.roll(x, LANES - 1, axis)
+
+    def left_of(x):
+        return pltpu.roll(x, 1, axis)
+
+    def below(xs):
+        return xs[1:] + [pltpu.roll(xs[0], HALF, axis)]
+
+    def above(xs):
+        return [pltpu.roll(xs[-1], HALF, axis)] + xs[:-1]
+
+    last = QUARTERS - 1
+    conduct = [jnp.exp(p) for p in perm_log]
+    half_cols = [jnp.where(inner_col, 0.5 * harmonic(c, right_of(c)), 0.0) for c in conduct]
+    half_rows = [0.5 * harmonic(c, d) for c, d in zip(conduct, below(conduct))]
+    half_rows[last] = jnp.where(upper, half_rows[last], 0.0)
+    factor = [TIME_STEP / p for p in porosity]
+    gain = [INJECT_RATE * w for w in well]
+    begin = [jnp.broadcast_to(s, p.shape) for s, p in zip(start, perm_log)]
+    height = begin
+    for _ in range(STEPS):
+        level = [h + t for h, t in zip(height, top)]
+        flux_cols = [
+            k * (h + right_of(h)) * (s - right_of(s))
+            for k, h, s in zip(half_cols, height, level)
+        ]
+        flux_rows = [
+            k * (h + g) * (s - r)
+            for k, h, g, s, r in zip(half_rows, height, below(height), level, below(level))
+        ]
+        height = [
+            h + f * (left_of(c) - c + a - r + g)
+            for h, f, c, a, r, g in zip(
+                height, factor, flux_cols, above(flux_rows), flux_rows, gain
+            )
+        ]
+    return [h - b for h, b in zip(height, begin)]
+
+
+def dot(a, b, dims):
+    return lax.dot_general(
+        a, b, (dims, ((), ())), precision=HIGHEST, preferred_element_type=jnp.float32
+    )
+
+
+def pivot_rows(pivot, rows):
+    r0, r1, r2, r3 = rows
+    p, q, s = pivot[0][0], pivot[0][1], pivot[1][1]
+    inverse = 1.0 / (p * s - q * q)
+    i00, i01, i11 = s * inverse, -q * inverse, p * inverse
+    c0, c1, e0, e1 = pivot[0][2], pivot[1][2], pivot[0][3], pivot[1][3]
+    y0, y1 = i00 * r0 + i01 * r1, i01 * r0 + i11 * r1
+    f0, f1 = i00 * c0 + i01 * c1, i01 * c0 + i11 * c1
+    g0, g1 = i00 * e0 + i01 * e1, i01 * e0 + i11 * e1
+    s22 = pivot[2][2] - (c0 * f0 + c1 * f1)
+    s23 = pivot[2][3] - (c0 * g0 + c1 * g1)
+    s33 = pivot[3][3] - (e0 * g0 + e1 * g1)
+    z2 = r2 - (c0 * y0 + c1 * y1)
+    z3 = r3 - (e0 * y0 + e1 * y1)
+    second = 1.0 / (s22 * s33 - s23 * s23)
+    u2 = (s33 * z2 - s23 * z3) * second
+    u3 = (s22 * z3 - s23 * z2) * second
+    return [y0 - f0 * u2 - g0 * u3, y1 - f1 * u2 - g1 * u3, u2, u3]
+
+
+def eliminate(gram, cross):
+    size = gram.shape[0]
+    work = jnp.concatenate([gram, cross], axis=1)
+    width = work.shape[1]
+    strips = [work[b : b + SUBLANES] for b in range(0, size, SUBLANES)]
+    line = lax.broadcasted_iota(jnp.int32, (SUBLANES, width), 0)
+    step = 4
+    for k in range(0, size, step):
+        columns = [
+            [jnp.broadcast_to(s[:, k + i : k + i + 1], s.shape) for i in range(step)]
+            for s in strips
+        ]
+        home, at = k // SUBLANES, k % SUBLANES
+        rows = [strips[home][at + i : at + i + 1] for i in range(step)]
+        pivot = [
+            [columns[home][j][at + i : at + i + 1] for j in range(step)] for i in range(step)
+        ]
+        solved = pivot_rows(pivot, rows)
+        following = []
+        for b, s in enumerate(strips):
+            c = columns[b]
+            if b == home:
+                for i in range(step):
+                    s = jnp.where(line == at + i, solved[i], s)
+                fixed = (line >= at) & (line < at + step)
+                c = [jnp.where(fixed, 0.0, x) for x in c]
+            s = s - ((c[0] * solved[0] + c[1] * solved[1]) + (c[2] * solved[2] + c[3] * solved[3]))
+            following.append(s)
+        strips = following
+    return jnp.concatenate(strips, axis=0)[:, size:]
+
+
+def mixing_of(predicted, innovation, error):
+    members = predicted.shape[0]
+    root = math.sqrt(members - 1.0)
+    scaled = (predicted - jnp.mean(predicted, axis=0, keepdims=True)) / (error * root)
+    both = dot(scaled, jnp.concatenate([scaled, innovation], axis=0), ((1,), (1,)))
+    gram, cross = both[:, :members], both[:, members:]
+    one = lax.broadcasted_iota(jnp.int32, gram.shape, 0)
+    two = lax.broadcasted_iota(jnp.int32, gram.shape, 1)
+    weights = eliminate(jnp.where(one == two, gram + INFLATION, gram), cross)
+    return (weights - jnp.mean(weights, axis=0, keepdims=True)) / root
+
+
+def local_kernel(
+    count,
+    perm_hbm,
+    start_hbm,
+    top_hbm,
+    porosity_hbm,
+    well_hbm,
+    cells_hbm,
+    observed_hbm,
+    error_hbm,
+    noise_hbm,
+    first_own,
+    patch_own,
+    patch,
+    mark,
+    perm_ref,
+    start_ref,
+    top_ref,
+    porosity_ref,
+    well_ref,
+    cells_ref,
+    observed_ref,
+    error_ref,
+    noise_ref,
+    stack,
+    folded,
+    load_sem,
+):
+    held, rows, cols = perm_ref.shape
+    nobs = error_ref.shape[1]
+
+    loads = [
+        pltpu.make_async_copy(source, target, load_sem.at[index])
+        for index, (source, target) in enumerate(
+            [
+                (perm_hbm, perm_ref),
+                (start_hbm, start_ref),
+                (top_hbm, top_ref),
+                (porosity_hbm, porosity_ref),
+                (well_hbm, well_ref),
+                (cells_hbm, cells_ref),
+                (observed_hbm, observed_ref),
+                (error_hbm, error_ref),
+                (noise_hbm, noise_ref),
+            ]
+        )
+    ]
+    for load in loads:
+        load.start()
+
+    for load in loads:
+        load.wait()
+
+    for strip in range(cols // LANES):
+        part = slice(strip * LANES, (strip + 1) * LANES)
+        fields = [perm_ref[member, :, part] for member in range(held)]
+        fields += [start_ref[:, part], top_ref[:, part], porosity_ref[:, part]]
+        fields += [well_ref[:, part].astype(jnp.float32)]
+        for index, field in enumerate(fields):
+            stack[strip, pl.ds(index, rows, stride=FIELDS), :] = field
+
+    lane = lax.broadcasted_iota(jnp.int32, (QUARTERS * FIELDS, LANES), 1)
+    quarter = lax.broadcasted_iota(jnp.int32, (QUARTERS * FIELDS, LANES), 0) // FIELDS
+    flat = quarter * LANES + lane
+    slot_of = (lane % HALF) // SIDE
+    upper = lane < HALF
+
+    def gather(chunk, cycle):
+        total, marks = None, jnp.zeros(lane.shape, jnp.float32)
+        for slot in range(SIDE):
+            cell = cells_ref[cycle, chunk * SIDE + slot]
+            row, col = lax.div(cell, cols), lax.rem(cell, cols)
+            row0 = jnp.clip(row - STEPS, 0, rows - SIDE)
+            col0 = jnp.clip(col - STEPS, 0, cols - SIDE)
+            low = lax.div(col0, LANES)
+            high = jnp.minimum(low + 1, cols // LANES - 1)
+            within = col0 - low * LANES
+            at = pl.multiple_of(row0 * FIELDS, FIELDS)
+            left = stack[low, pl.ds(at, SIDE * FIELDS), :]
+            right = stack[high, pl.ds(at, SIDE * FIELDS), :]
+            inside = lane >= within
+            here = quarter.shape[0]
+            one = jnp.where(inside, left[:here], right[:here])
+            two = jnp.where(inside, left[here:], right[here:])
+            turn = lax.rem(slot * SIDE + LANES - within, LANES)
+            one = pltpu.roll(one, turn, 1)
+            two = pltpu.roll(two, lax.rem(turn + HALF, LANES), 1)
+            moved = jnp.where(upper, one, two)
+            total = moved if total is None else jnp.where(slot_of == slot, moved, total)
+            down, along = row - row0, col - col0
+            spot = lax.rem(down, QUARTERS) * LANES + lax.div(down, QUARTERS) * HALF
+            marks = jnp.where(flat == spot + slot * SIDE + along, 1.0, marks)
+        at = pl.ds(pl.multiple_of(chunk * (QUARTERS * FIELDS), FIELDS), QUARTERS * FIELDS)
+        if cycle == 1:
+            patch[at, :] = total
+            mark[at, :] = marks
+        return total, marks
+
+    def first_chunk(chunk, carry):
+        total, marks = gather(chunk, 0)
+        parts = [total[v * FIELDS : (v + 1) * FIELDS] for v in range(QUARTERS)]
+        marked = [marks[v * FIELDS : (v + 1) * FIELDS] for v in range(QUARTERS)]
+        lines = [[p[held + f : held + f + 1] for p in parts] for f in range(4)]
+        change = patch_plume(parts, *lines)
+        sums = sum(jnp.where(m > 0.0, c, 0.0) for c, m in zip(change, marked))
+        folded[pl.ds(pl.multiple_of(chunk * FIELDS, FIELDS), FIELDS), :] = sums
+        return carry
+
+    lax.fori_loop(0, count, first_chunk, 0, unroll=2)
+
+    one = lax.broadcasted_iota(jnp.int32, (LANES, nobs), 0)
+    two = lax.broadcasted_iota(jnp.int32, (LANES, nobs), 1)
+    spread = dot(
+        folded[...], jnp.where((one % HALF) // SIDE == two % SIDE, 1.0, 0.0), ((1,), (0,))
+    ).reshape(count, FIELDS, nobs)
+    turn = lax.broadcasted_iota(jnp.int32, spread.shape, 0)
+    place = lax.broadcasted_iota(jnp.int32, spread.shape, 2)
+    predicted = jnp.sum(jnp.where(place // SIDE == turn, spread, 0.0), axis=0)[:held]
+    error = error_ref[...]
+    first_own[0:held, :] = predicted
+    first_own[held : 2 * held, :] = make_innovation(
+        predicted, observed_ref[0:1, :], error, noise_ref[0]
+    )
+    first_own[2 * held : 3 * held, :] = make_innovation(
+        jnp.zeros_like(predicted), observed_ref[1:2, :], error, noise_ref[1]
+    )
+    first_own[3 * held : 4 * held, :] = jnp.zeros_like(predicted)
+
+    def second_chunk(chunk, carry):
+        total, _ = gather(chunk, 1)
+        for pair in range(QUARTERS // 2):
+            at = 2 * pair * FIELDS
+            patch_own[chunk, pair] = jnp.concatenate(
+                [total[at : at + held], total[at + FIELDS : at + FIELDS + held]], axis=0
+            )
+        return carry
+
+    lax.fori_loop(0, count, second_chunk, 0, unroll=2)
+
+
+def ensemble_kernel(
+    count,
+    perm_ref,
+    first_own,
+    patch_own,
+    patch,
+    mark,
+    error_ref,
+    out_ref,
+    first_all,
+    patch_all,
+    pred_all,
+    block,
+    mixed,
+    send_sem,
+    recv_sem,
+    local_sem,
+):
+    held, rows, cols = perm_ref.shape
+    members = held * count
+    nobs = error_ref.shape[1]
+    deep = count * FIELDS
+    me = lax.axis_index("member")
+    _, tall, wide = block.shape
+    across = cols // wide
+
+    def cells_of(ref, device):
+        return ref.at[
+            :,
+            pl.ds(pl.multiple_of((device // across) * tall, tall), tall),
+            pl.ds(pl.multiple_of((device % across) * wide, wide), wide),
+        ]
+
+    def members_of(ref, device):
+        return ref.at[pl.ds(device * held, held)]
+
+    def obs_of(ref, device):
+        return ref.at[pl.ds(pl.multiple_of(device * SIDE, SIDE), SIDE)]
+
+    ways = [
+        (lambda peer: first_own, lambda owner: first_all.at[owner]),
+        (lambda peer: patch_own.at[peer], lambda owner: patch_all.at[owner]),
+        (lambda peer: cells_of(perm_ref, peer), lambda owner: members_of(block, owner)),
+        (lambda peer: obs_of(pred_all, me), lambda owner: obs_of(pred_all, owner)),
+        (lambda peer: members_of(mixed, peer), lambda owner: cells_of(out_ref, owner)),
+    ]
+
+    def transfer(kind, peer, owner, slot):
+        source, target = ways[kind]
+        return pltpu.make_async_remote_copy(
+            src_ref=source(peer),
+            dst_ref=target(owner),
+            send_sem=send_sem.at[kind, slot],
+            recv_sem=recv_sem.at[kind, slot],
+            device_id={"member": peer},
+            device_id_type=MESH,
+        )
+
+    def each(body, low=1, high=count):
+        def step(j, carry):
+            body(j)
+            return carry
+
+        lax.fori_loop(low, high, step, 0)
+
+    def send(kind, low=1, high=count):
+        each(lambda j: transfer(kind, lax.rem(me + j, count), me, j).start(), low, high)
+
+    def receive(kind):
+        each(lambda j: transfer(kind, me, lax.rem(me + count - j, count), j).wait_recv())
+
+    def sent(kind):
+        each(lambda j: transfer(kind, lax.rem(me + j, count), me, j).wait_send())
+
+    barrier = pltpu.get_barrier_semaphore()
+    each(
+        lambda j: pl.semaphore_signal(
+            barrier,
+            inc=1,
+            device_id={"member": lax.rem(me + j, count)},
+            device_id_type=MESH,
+        )
+    )
+    pl.semaphore_wait(barrier, count - 1)
+    send(0)
+    send(1)
+    send(2)
+    own_in = pltpu.make_async_copy(cells_of(perm_ref, me), members_of(block, me), local_sem.at[0])
+    own_in.start()
+    first_all[me] = first_own[...]
+    patch_all[me] = patch_own[me]
+    error = error_ref[...]
+
+    depth = first_own.shape[0]
+    line = lax.broadcasted_iota(jnp.int32, (members, count * depth), 0)
+    spot = lax.broadcasted_iota(jnp.int32, (members, count * depth), 1)
+    home = (line // held) * depth + line % held
+
+    receive(0)
+    whole = first_all[...].reshape(count * depth, nobs)
+
+    def pick(offset):
+        return dot(jnp.where(spot == home + offset, 1.0, 0.0), whole, ((1,), (0,)))
+
+    first_mix = mixing_of(pick(0), pick(held), error)
+    base = pick(2 * held)
+
+    receive(1)
+    line2 = lax.broadcasted_iota(jnp.int32, (members, deep), 0)
+    spot2 = lax.broadcasted_iota(jnp.int32, (members, deep), 1)
+    home2 = (line2 // held) * FIELDS + line2 % held
+    at = pl.multiple_of(me * (QUARTERS * FIELDS), FIELDS)
+    perms, lines, marked = [], [[], [], [], []], []
+    for v in range(QUARTERS):
+        choose = jnp.where(spot2 == home2 + (v % 2) * held, 1.0, 0.0)
+        values = patch_all[:, v // 2].reshape(deep, LANES)
+        prior = dot(choose, values, ((1,), (0,)))
+        perms.append(prior + dot(first_mix, prior, ((0,), (0,))))
+        own = patch[pl.ds(at + v * FIELDS, FIELDS), :]
+        for f in range(4):
+            lines[f].append(own[held + f : held + f + 1])
+        marked.append(mark[pl.ds(at + v * FIELDS, FIELDS), :][0:1])
+    change = patch_plume(perms, *lines)
+    sums = sum(jnp.where(m > 0.0, c, 0.0) for c, m in zip(change, marked))
+    one = lax.broadcasted_iota(jnp.int32, (SIDE, LANES), 0)
+    two = lax.broadcasted_iota(jnp.int32, (SIDE, LANES), 1)
+    fresh = dot(jnp.where((two % HALF) // SIDE == one, 1.0, 0.0), sums, ((1,), (1,)))
+    pred_all[pl.ds(pl.multiple_of(me * SIDE, SIDE), SIDE), :] = jnp.concatenate(
+        [fresh, jnp.zeros((SIDE, pred_all.shape[1] - members), jnp.float32)], axis=1
+    )
+    send(3)
+    receive(3)
+    table = pred_all[...].T[:members]
+    second_mix = mixing_of(table, base - table / error, error)
+    mixing = first_mix + second_mix + dot(first_mix, second_mix, ((1,), (0,)))
+
+    receive(2)
+    own_in.wait()
+    for r in range(tall):
+        prior = block[:, r, :]
+        mixed[:, r, :] = prior + dot(mixing, prior, ((0,), (0,)))
+    send(4)
+    own_out = pltpu.make_async_copy(members_of(mixed, me), cells_of(out_ref, me), local_sem.at[1])
+    own_out.start()
+    for kind in range(4):
+        sent(kind)
+    own_out.wait()
+    receive(4)
+    sent(4)
+
+
+def patch_device(count, perm, start, top, porosity, well, cells, observed, error, noise):
+    held, rows, cols = perm.shape
+    nobs = observed.shape[1]
+    members = held * count
+    wide = cols // ((count * SIDE) // rows)
+    error = error.reshape(1, nobs)
+    operands = (perm, start, top, porosity, well, cells, observed, error, noise)
+    local = [
+        (pltpu.SMEM if x is cells else pltpu.VMEM)(x.shape, x.dtype) for x in operands
+    ]
+    vmem = pl.BlockSpec(memory_space=pltpu.VMEM)
+    grant = 32 * 1024 * 1024
+
+    def scratch(*shape):
+        return pltpu.VMEM(shape, jnp.float32)
+
+    found = [
+        (4 * held, nobs),
+        (count, QUARTERS // 2, 2 * held, LANES),
+        (count * QUARTERS * FIELDS, LANES),
+        (count * QUARTERS * FIELDS, LANES),
+    ]
+    gathered = pl.pallas_call(
+        functools.partial(local_kernel, count),
+        out_shape=[jax.ShapeDtypeStruct(shape, jnp.float32) for shape in found],
+        in_specs=[pl.BlockSpec(memory_space=pl.ANY)] * len(operands),
+        out_specs=[vmem] * len(found),
+        scratch_shapes=local
+        + [
+            scratch(cols // LANES, rows * FIELDS, LANES),
+            scratch(count * FIELDS, LANES),
+            pltpu.SemaphoreType.DMA((len(operands),)),
+        ],
+        compiler_params=pltpu.CompilerParams(vmem_limit_bytes=grant),
+    )(*operands)
+    return pl.pallas_call(
+        functools.partial(ensemble_kernel, count),
+        out_shape=jax.ShapeDtypeStruct(perm.shape, jnp.float32),
+        in_specs=[vmem] * (len(found) + 2),
+        out_specs=vmem,
+        scratch_shapes=[
+            scratch(count, *found[0]),
+            scratch(*found[1]),
+            scratch(nobs, LANES),
+            scratch(members, SIDE, wide),
+            scratch(members, SIDE, wide),
+            pltpu.SemaphoreType.DMA((KINDS, count)),
+            pltpu.SemaphoreType.DMA((KINDS, count)),
+            pltpu.SemaphoreType.DMA((2,)),
+        ],
+        compiler_params=pltpu.CompilerParams(
+            collective_id=0, has_side_effects=True, vmem_limit_bytes=grant
+        ),
+    )(perm, *gathered, error)
+
+
+def fits(count, held, rows, cols, nobs):
+    return (
+        2 * held == FIELDS
+        and 2 * count * held == LANES
+        and nobs == LANES
+        and nobs == count * SIDE
+        and rows % SIDE == 0
+        and (count * SIDE) % rows == 0
+        and cols % ((count * SIDE // rows) * LANES) == 0
+    )
+
+
+def device_program(perm, *rest):
+    count = lax.axis_size("member")
+    held, rows, cols = perm.shape
+    if fits(count, held, rows, cols, rest[5].shape[1]):
+        return patch_device(count, perm, *rest)
+    return on_device(perm, *rest)
+
+
 def solution(mesh):
     return jax.shard_map(
-        on_device,
+        device_program,
         mesh=mesh,
         in_specs=(
             P(("region", "member"), None, None),

time: 207 us -> 61.9 us (0.30); the launches traced: 205 us -> 61.6 us
  blocking collectives: 92.2 us -> 0 us
  Pallas kernels: 0 us -> 54.1 us
  other arithmetic: 36.6 us -> 0 us
  local copies, waits for them, and re-layouts: 39 us -> 7.51 us
  starting transfers between devices: 19.5 us -> 0 us
  waiting for transfers between devices: 14.1 us -> 0 us
  matrix products: 2.8 us -> 0 us
    all_gather x4 -> x0, blocking collectives: 72.5 us -> none  [the longest x2 36.5 us: ensemble_solve(): lax.all_gather(innovation, 'member', axis=0, tiled=True)]
    pallas_call x0 -> x2, Pallas kernels: none -> 54.1 us  [the longest x1 42.4 us: patch_device(): pl.pallas_call(functools.partial(ensemble_kernel, count), out_shape=jax.S...]
    another operation x10 -> x0, other arithmetic: 24.4 us -> none  [the longest x6 13.2 us: solve_weights(): factor = jnp.linalg.cholesky(full)]
    all_to_all x1 -> x0, blocking collectives: 19.7 us -> none  [on_device(): lax.all_to_all(cell_major, 'member', split_axis=0, concat_axis=1, tiled=T...]
    all_to_all x3 -> x0, starting transfers between devices: 19.5 us -> none  [the longest x2 13 us: on_device(): lax.all_to_all(perm.reshape(held_count, map_rows * map_cols), 'member', s...]
    sub x2 -> x0, local copies, waits for them, and re-layouts: 17.3 us -> none  [on_device(): change = (height - start_height).reshape(held_count, map_rows * map_cols)]
    all_to_all x3 -> x0, waiting for transfers between devices: 14.1 us -> none  [the longest x1 14.1 us: on_device(): lax.all_to_all(cell_major, 'member', split_axis=0, concat_axis=1, tiled=T...]
    gather x2 -> x0, local copies, waits for them, and re-layouts: 12.8 us -> none  [on_device(): predicted = jnp.take(change, obs_cells[cycle_index], axis=1)]
  transfers between devices with their start and end apart: 3 -> 0, of which waited for: 1 -> 0; matrix products, arithmetic and copies ran while one was open for 22% -> 0% of each run, Pallas kernels for 0% -> 0%
where the time goes in v2:
time: 61.9 us; the launch traced here: 61.6 us
  Pallas kernels  54.1 us (87%)
  local copies, waits for them, and re-layouts  7.51 us (12%)
    pallas_call x1, Pallas kernels, patch_device(): pl.pallas_call(functools.partial(ensemble_kernel, count), out_shape=jax.S...  42.4 us
    pallas_call x1, Pallas kernels, patch_device(): pl.pallas_call(functools.partial(local_kernel, count), out_shape=[jax.Sha...  11.6 us
    unnamed x19, local copies, waits for them, and re-layouts  7.51 us

profile of v2, /device:TPU:9, one launch (start us, length us, event | category | flops | bytes accessed | tf_op | source)
XLA Modules:
  0.0 61.6 jit_solution(9471724097686203746)
XLA Ops:
  0.0 0.0 copy-start.6
  0.0 0.0 copy-start.7
  0.0 0.7 %copy-done.6 = f32[128]{0:T(128)S(1)} copy-done((f32[128]{0:T(128)S(1)}, f32[128]{0:T(128)}, u32[]{:S(2)}) %copy-start.6) | copy-done | bytes 536
  0.7 0.0 copy-done.7
  0.7 0.0 copy-start
  0.7 1.0 %copy-done = f32[4,64,512]{2,1,0:T(8,128)S(1)} copy-done((f32[4,64,512]{2,1,0:T(8,128)S(1)}, f32[4,64,512]{2,1,0:T(8,128)}, u32[]{:S(2)}) %copy-start) | copy-done | bytes 524312
  1.7 0.0 copy-start.1
  1.7 0.9 %copy-done.1 = f32[64,512]{1,0:T(8,128)S(1)} copy-done((f32[64,512]{1,0:T(8,128)S(1)}, f32[64,512]{1,0:T(8,128)}, u32[]{:S(2)}) %copy-start.1) | copy-done | bytes 131096
  2.6 0.0 copy-start.2
  2.6 0.9 %copy-done.2 = f32[64,512]{1,0:T(8,128)S(1)} copy-done((f32[64,512]{1,0:T(8,128)S(1)}, f32[64,512]{1,0:T(8,128)}, u32[]{:S(2)}) %copy-start.2) | copy-done | bytes 131096
  3.5 0.0 copy-start.3
  3.5 0.9 %copy-done.3 = f32[64,512]{1,0:T(8,128)S(1)} copy-done((f32[64,512]{1,0:T(8,128)S(1)}, f32[64,512]{1,0:T(8,128)}, u32[]{:S(2)}) %copy-start.3) | copy-done | bytes 131096
  4.5 0.0 copy-start.4
  4.5 0.9 %copy-done.4 = s32[64,512]{1,0:T(8,128)S(1)} copy-done((s32[64,512]{1,0:T(8,128)S(1)}, s32[64,512]{1,0:T(8,128)}, u32[]{:S(2)}) %copy-start.4) | copy-done | bytes 131096
  5.4 0.0 copy-start.5
  5.4 0.7 %copy-done.5 = s32[2,4,128]{2,1,0:T(4,128)S(1)} copy-done((s32[2,4,128]{2,1,0:T(4,128)S(1)}, s32[2,4,128]{2,1,0:T(4,128)}, u32[]{:S(2)}) %copy-start.5) | copy-done | bytes 4120
  6.0 0.0 copy-start.8
  6.0 0.7 %copy-done.8 = f32[2,128]{1,0:T(2,128)S(1)} copy-done((f32[2,128]{1,0:T(2,128)S(1)}, f32[2,128]{1,0:T(2,128)}, u32[]{:S(2)}) %copy-start.8) | copy-done | bytes 1048
  6.7 11.6 %shard_map.91 = (f32[16,128]{1,0:T(8,128)S(1)}, f32[16,2,8,128]{3,2,1,0:T(8,128)S(1)}, f32[512,128]{1,0:T(8,128)S(1)}, f32[512,128]{1,0:T(8,128)S(1)}) custom-call(f32[4,64,512]{2,1,0:T(8,128)S(1)} %copy-done, f32[64,512]{1,0:T(8,128)S(1)} %copy-done.1, f32[64,512]{1,0:T(8,128)S(1)} %copy-done.2, f32[64,512]{1,0:T(8,128)S(1)} %copy-done.3, ...), custom_call_target="tpu_custom_call" | custom-call | tf_op jit(solution)/shard_map/pallas_call | solution.py:572
  18.4 42.4 %shard_map.92 = f32[4,64,512]{2,1,0:T(8,128)S(1)} custom-call(f32[4,64,512]{2,1,0:T(8,128)S(1)} %copy-done, f32[16,128]{1,0:T(8,128)S(1)} %get-tuple-element.9.first_own, f32[16,2,8,128]{3,2,1,0:T(8,128)S(1)} %get-tuple-element.10.patch_own, f32[512,128]{1,0:T(8,128)S(1)} %get-tuple-element.11.patch, f32[512,128]{1,0:T(8,128)S(1)} %get-tuple-element.12.mark, ...), custom_call_target="tpu_custom_call" | custom-call | tf_op jit(solution)/shard_map/pallas_call | solution.py:585
  60.8 0.8 %copy.11 = f32[4,64,512]{2,1,0:T(8,128)} copy(f32[4,64,512]{2,1,0:T(8,128)S(1)} %shard_map.92) | data formatting | bytes 1048576
Async XLA Ops:
  0.0 0.7 %copy-start.6 = (f32[128]{0:T(128)S(1)}, f32[128]{0:T(128)}, u32[]{:S(2)}) copy-start(f32[128]{0:T(128)} %param.16) | copy-start | bytes 1540
  0.0 0.7 %copy-start.7 = (s32[2,128]{1,0:T(2,128)S(1)}, s32[2,128]{1,0:T(2,128)}, u32[]{:S(2)}) copy-start(s32[2,128]{1,0:T(2,128)} %cells_hbm.1) | copy-start | bytes 3076
  0.7 1.0 %copy-start = (f32[4,64,512]{2,1,0:T(8,128)S(1)}, f32[4,64,512]{2,1,0:T(8,128)}, u32[]{:S(2)}) copy-start(f32[4,64,512]{2,1,0:T(8,128)} %perm_ref.1) | copy-start | bytes 1572868
  1.7 0.9 %copy-start.1 = (f32[64,512]{1,0:T(8,128)S(1)}, f32[64,512]{1,0:T(8,128)}, u32[]{:S(2)}) copy-start(f32[64,512]{1,0:T(8,128)} %start_hbm.1) | copy-start | bytes 393220
  2.6 0.9 %copy-start.2 = (f32[64,512]{1,0:T(8,128)S(1)}, f32[64,512]{1,0:T(8,128)}, u32[]{:S(2)}) copy-start(f32[64,512]{1,0:T(8,128)} %top_hbm.1) | copy-start | bytes 393220
  3.5 0.9 %copy-start.3 = (f32[64,512]{1,0:T(8,128)S(1)}, f32[64,512]{1,0:T(8,128)}, u32[]{:S(2)}) copy-start(f32[64,512]{1,0:T(8,128)} %porosity_hbm.1) | copy-start | bytes 393220
  4.5 0.9 %copy-start.4 = (s32[64,512]{1,0:T(8,128)S(1)}, s32[64,512]{1,0:T(8,128)}, u32[]{:S(2)}) copy-start(s32[64,512]{1,0:T(8,128)} %well_hbm.1) | copy-start | bytes 393220
  5.4 0.7 %copy-start.5 = (s32[2,4,128]{2,1,0:T(4,128)S(1)}, s32[2,4,128]{2,1,0:T(4,128)}, u32[]{:S(2)}) copy-start(s32[2,4,128]{2,1,0:T(4,128)} %noise_hbm.1) | copy-start | bytes 12292
  6.0 0.7 %copy-start.8 = (f32[2,128]{1,0:T(2,128)S(1)}, f32[2,128]{1,0:T(2,128)}, u32[]{:S(2)}) copy-start(f32[2,128]{1,0:T(2,128)} %observed_hbm.1) | copy-start | bytes 3076

commit v3 on v2

--- a/solution.py
+++ b/solution.py
@@ -16,7 +16,6 @@
 QUARTERS = SIDE // 2
 FIELDS = 8
 SUBLANES = 8
-KINDS = 5
 
 STEPS = 3
 CYCLES = 2
@@ -264,28 +263,24 @@
     porosity_hbm,
     well_hbm,
     cells_hbm,
-    observed_hbm,
-    error_hbm,
-    noise_hbm,
-    first_own,
+    patch_one,
+    mark_one,
     patch_own,
-    patch,
-    mark,
+    patch_two,
+    mark_two,
     perm_ref,
     start_ref,
     top_ref,
     porosity_ref,
     well_ref,
     cells_ref,
-    observed_ref,
-    error_ref,
-    noise_ref,
     stack,
-    folded,
+    patch_all_two,
+    mark_all_two,
     load_sem,
 ):
     held, rows, cols = perm_ref.shape
-    nobs = error_ref.shape[1]
+    me = lax.axis_index("member")
 
     loads = [
         pltpu.make_async_copy(source, target, load_sem.at[index])
@@ -297,9 +292,6 @@
                 (porosity_hbm, porosity_ref),
                 (well_hbm, well_ref),
                 (cells_hbm, cells_ref),
-                (observed_hbm, observed_ref),
-                (error_hbm, error_ref),
-                (noise_hbm, noise_ref),
             ]
         )
     ]
@@ -317,45 +309,201 @@
         for index, field in enumerate(fields):
             stack[strip, pl.ds(index, rows, stride=FIELDS), :] = field
 
-    lane = lax.broadcasted_iota(jnp.int32, (QUARTERS * FIELDS, LANES), 1)
-    quarter = lax.broadcasted_iota(jnp.int32, (QUARTERS * FIELDS, LANES), 0) // FIELDS
-    flat = quarter * LANES + lane
-    slot_of = (lane % HALF) // SIDE
-    upper = lane < HALF
-
-    def gather(chunk, cycle):
-        total, marks = None, jnp.zeros(lane.shape, jnp.float32)
+    lane = lax.broadcasted_iota(jnp.int32, (SIDE * FIELDS, LANES), 1)
+    short = (QUARTERS * FIELDS, LANES)
+    low_lane = lax.broadcasted_iota(jnp.int32, short, 1)
+    flat = lax.broadcasted_iota(jnp.int32, short, 0) // FIELDS * LANES + low_lane
+    slot_of = lane // SIDE
+    upper = low_lane < HALF
+    cols_bits, lane_bits = cols.bit_length() - 1, LANES.bit_length() - 1
+
+    def gather(chunk, cycle, patches, marked):
+        total, marks = None, jnp.zeros(short, jnp.float32)
         for slot in range(SIDE):
             cell = cells_ref[cycle, chunk * SIDE + slot]
-            row, col = lax.div(cell, cols), lax.rem(cell, cols)
+            row, col = cell >> cols_bits, cell & (cols - 1)
             row0 = jnp.clip(row - STEPS, 0, rows - SIDE)
             col0 = jnp.clip(col - STEPS, 0, cols - SIDE)
-            low = lax.div(col0, LANES)
+            low = col0 >> lane_bits
             high = jnp.minimum(low + 1, cols // LANES - 1)
-            within = col0 - low * LANES
+            within = col0 & (LANES - 1)
             at = pl.multiple_of(row0 * FIELDS, FIELDS)
             left = stack[low, pl.ds(at, SIDE * FIELDS), :]
             right = stack[high, pl.ds(at, SIDE * FIELDS), :]
-            inside = lane >= within
-            here = quarter.shape[0]
-            one = jnp.where(inside, left[:here], right[:here])
-            two = jnp.where(inside, left[here:], right[here:])
-            turn = lax.rem(slot * SIDE + LANES - within, LANES)
-            one = pltpu.roll(one, turn, 1)
-            two = pltpu.roll(two, lax.rem(turn + HALF, LANES), 1)
-            moved = jnp.where(upper, one, two)
+            window = jnp.where(lane >= within, left, right)
+            moved = pltpu.roll(window, (slot * SIDE - within) & (LANES - 1), 1)
             total = moved if total is None else jnp.where(slot_of == slot, moved, total)
             down, along = row - row0, col - col0
-            spot = lax.rem(down, QUARTERS) * LANES + lax.div(down, QUARTERS) * HALF
-            marks = jnp.where(flat == spot + slot * SIDE + along, 1.0, marks)
-        at = pl.ds(pl.multiple_of(chunk * (QUARTERS * FIELDS), FIELDS), QUARTERS * FIELDS)
-        if cycle == 1:
-            patch[at, :] = total
-            mark[at, :] = marks
-        return total, marks
+            spot = (down & (QUARTERS - 1)) * LANES + (down // QUARTERS) * HALF + along
+            marks = jnp.where(flat == spot + slot * SIDE, 1.0, marks)
+        half = short[0]
+        total = jnp.where(upper, total[:half], pltpu.roll(total[half:], HALF, 1))
+        at = pl.ds(pl.multiple_of(chunk * half, FIELDS), half)
+        patches[at, :] = total
+        marked[at, :] = marks
+        return total
 
     def first_chunk(chunk, carry):
-        total, marks = gather(chunk, 0)
+        gather(chunk, 0, patch_one, mark_one)
+        return carry
+
+    def second_chunk(chunk, carry):
+        total = gather(chunk, 1, patch_all_two, mark_all_two)
+        rows_of = [total[v * FIELDS : v * FIELDS + held] for v in range(QUARTERS)]
+        depth = QUARTERS * held
+        at = pl.ds(pl.multiple_of(chunk * depth, FIELDS), depth)
+        patch_own[at, :] = jnp.concatenate(rows_of, axis=0)
+        return carry
+
+    lax.fori_loop(0, count, second_chunk, 0, unroll=2)
+    lax.fori_loop(0, count, first_chunk, 0, unroll=2)
+    own = pl.ds(pl.multiple_of(me * short[0], FIELDS), short[0])
+    patch_two[...] = patch_all_two[own, :]
+    mark_two[...] = mark_all_two[own, :]
+
+
+def ensemble_kernel(
+    count,
+    perm_ref,
+    patch_one_hbm,
+    mark_one_hbm,
+    patch_own,
+    patch_two_hbm,
+    mark_two_hbm,
+    observed_hbm,
+    error_hbm,
+    noise_hbm,
+    out_ref,
+    patch_one,
+    mark_one,
+    patch_two,
+    mark_two,
+    observed_ref,
+    error_ref,
+    noise_ref,
+    folded,
+    first_own,
+    first_all,
+    patch_all,
+    pred_all,
+    block,
+    mixed,
+    send_sem,
+    recv_sem,
+    load_sem,
+):
+    held, rows, cols = perm_ref.shape
+    members = held * count
+    nobs = error_ref.shape[1]
+    depth = first_own.shape[0]
+    me = lax.axis_index("member")
+    tall, wide = block.shape[2:]
+    across = cols // wide
+
+    def cells_of(ref, device):
+        return ref.at[
+            :,
+            pl.ds(pl.multiple_of((device // across) * tall, tall), tall),
+            pl.ds(pl.multiple_of((device % across) * wide, wide), wide),
+        ]
+
+    def members_of(ref, device):
+        return ref.at[:, device]
+
+    def half_of(ref, device, half):
+        return ref.at[
+            :,
+            pl.ds(pl.multiple_of((device // across) * tall, tall), tall),
+            pl.ds(pl.multiple_of((device % across) * wide + half * LANES, LANES), LANES),
+        ]
+
+    def depth_of(ref, device):
+        return ref.at[pl.ds(pl.multiple_of(device * depth, depth), depth)]
+
+    def obs_of(ref, device):
+        return ref.at[pl.ds(pl.multiple_of(device * SIDE, SIDE), SIDE)]
+
+    ways = [
+        (lambda peer: first_own, lambda owner: depth_of(first_all, owner)),
+        (lambda peer: depth_of(patch_own, peer), lambda owner: depth_of(patch_all, owner)),
+        (lambda peer: cells_of(perm_ref, peer), lambda owner: members_of(block, owner)),
+        (lambda peer: obs_of(pred_all, me), lambda owner: obs_of(pred_all, owner)),
+    ]
+    for half in range(wide // LANES):
+        ways.append(
+            (
+                lambda peer, half=half: members_of(mixed.at[half], peer),
+                lambda owner, half=half: half_of(out_ref, owner, half),
+            )
+        )
+
+    def transfer(kind, peer, owner, slot):
+        source, target = ways[kind]
+        return pltpu.make_async_remote_copy(
+            src_ref=source(peer),
+            dst_ref=target(owner),
+            send_sem=send_sem.at[kind, slot],
+            recv_sem=recv_sem.at[kind, slot],
+            device_id={"member": peer},
+            device_id_type=MESH,
+        )
+
+    def each(body, low=1, high=count):
+        def step(j, carry):
+            body(j)
+            return carry
+
+        lax.fori_loop(low, high, step, 0)
+
+    def send(kind, low=1, high=count):
+        each(lambda j: transfer(kind, lax.rem(me + j, count), me, j).start(), low, high)
+
+    def receive(kind):
+        each(lambda j: transfer(kind, me, lax.rem(me + count - j, count), j).wait_recv())
+
+    def sent(kind):
+        each(lambda j: transfer(kind, lax.rem(me + j, count), me, j).wait_send())
+
+    loads = [
+        pltpu.make_async_copy(source, target, load_sem.at[index])
+        for index, (source, target) in enumerate(
+            [
+                (patch_one_hbm, patch_one),
+                (mark_one_hbm, mark_one),
+                (patch_two_hbm, patch_two),
+                (mark_two_hbm, mark_two),
+                (observed_hbm, observed_ref),
+                (error_hbm, error_ref),
+                (noise_hbm, noise_ref),
+                (cells_of(perm_ref, me), members_of(block, me)),
+                (depth_of(patch_own, me), depth_of(patch_all, me)),
+            ]
+        )
+    ]
+    for load in loads:
+        load.start()
+
+    barrier = pltpu.get_barrier_semaphore()
+    each(
+        lambda j: pl.semaphore_signal(
+            barrier,
+            inc=1,
+            device_id={"member": lax.rem(me + j, count)},
+            device_id_type=MESH,
+        )
+    )
+    for load in loads:
+        load.wait()
+    pl.semaphore_wait(barrier, count - 1)
+    third = (count + 1) // 3
+    send(1)
+    send(2, 1, third)
+
+    group = QUARTERS * FIELDS
+
+    def first_chunk(chunk, carry):
+        at = pl.ds(pl.multiple_of(chunk * group, group), group)
+        total, marks = patch_one[at, :], mark_one[at, :]
         parts = [total[v * FIELDS : (v + 1) * FIELDS] for v in range(QUARTERS)]
         marked = [marks[v * FIELDS : (v + 1) * FIELDS] for v in range(QUARTERS)]
         lines = [[p[held + f : held + f + 1] for p in parts] for f in range(4)]
@@ -383,141 +531,30 @@
         jnp.zeros_like(predicted), observed_ref[1:2, :], error, noise_ref[1]
     )
     first_own[3 * held : 4 * held, :] = jnp.zeros_like(predicted)
-
-    def second_chunk(chunk, carry):
-        total, _ = gather(chunk, 1)
-        for pair in range(QUARTERS // 2):
-            at = 2 * pair * FIELDS
-            patch_own[chunk, pair] = jnp.concatenate(
-                [total[at : at + held], total[at + FIELDS : at + FIELDS + held]], axis=0
-            )
-        return carry
-
-    lax.fori_loop(0, count, second_chunk, 0, unroll=2)
-
-
-def ensemble_kernel(
-    count,
-    perm_ref,
-    first_own,
-    patch_own,
-    patch,
-    mark,
-    error_ref,
-    out_ref,
-    first_all,
-    patch_all,
-    pred_all,
-    block,
-    mixed,
-    send_sem,
-    recv_sem,
-    local_sem,
-):
-    held, rows, cols = perm_ref.shape
-    members = held * count
-    nobs = error_ref.shape[1]
-    deep = count * FIELDS
-    me = lax.axis_index("member")
-    _, tall, wide = block.shape
-    across = cols // wide
-
-    def cells_of(ref, device):
-        return ref.at[
-            :,
-            pl.ds(pl.multiple_of((device // across) * tall, tall), tall),
-            pl.ds(pl.multiple_of((device % across) * wide, wide), wide),
-        ]
-
-    def members_of(ref, device):
-        return ref.at[pl.ds(device * held, held)]
-
-    def obs_of(ref, device):
-        return ref.at[pl.ds(pl.multiple_of(device * SIDE, SIDE), SIDE)]
-
-    ways = [
-        (lambda peer: first_own, lambda owner: first_all.at[owner]),
-        (lambda peer: patch_own.at[peer], lambda owner: patch_all.at[owner]),
-        (lambda peer: cells_of(perm_ref, peer), lambda owner: members_of(block, owner)),
-        (lambda peer: obs_of(pred_all, me), lambda owner: obs_of(pred_all, owner)),
-        (lambda peer: members_of(mixed, peer), lambda owner: cells_of(out_ref, owner)),
-    ]
-
-    def transfer(kind, peer, owner, slot):
-        source, target = ways[kind]
-        return pltpu.make_async_remote_copy(
-            src_ref=source(peer),
-            dst_ref=target(owner),
-            send_sem=send_sem.at[kind, slot],
-            recv_sem=recv_sem.at[kind, slot],
-            device_id={"member": peer},
-            device_id_type=MESH,
-        )
-
-    def each(body, low=1, high=count):
-        def step(j, carry):
-            body(j)
-            return carry
-
-        lax.fori_loop(low, high, step, 0)
-
-    def send(kind, low=1, high=count):
-        each(lambda j: transfer(kind, lax.rem(me + j, count), me, j).start(), low, high)
-
-    def receive(kind):
-        each(lambda j: transfer(kind, me, lax.rem(me + count - j, count), j).wait_recv())
-
-    def sent(kind):
-        each(lambda j: transfer(kind, lax.rem(me + j, count), me, j).wait_send())
-
-    barrier = pltpu.get_barrier_semaphore()
-    each(
-        lambda j: pl.semaphore_signal(
-            barrier,
-            inc=1,
-            device_id={"member": lax.rem(me + j, count)},
-            device_id_type=MESH,
-        )
-    )
-    pl.semaphore_wait(barrier, count - 1)
     send(0)
-    send(1)
-    send(2)
-    own_in = pltpu.make_async_copy(cells_of(perm_ref, me), members_of(block, me), local_sem.at[0])
-    own_in.start()
-    first_all[me] = first_own[...]
-    patch_all[me] = patch_own[me]
-    error = error_ref[...]
-
-    depth = first_own.shape[0]
-    line = lax.broadcasted_iota(jnp.int32, (members, count * depth), 0)
-    spot = lax.broadcasted_iota(jnp.int32, (members, count * depth), 1)
-    home = (line // held) * depth + line % held
+    send(2, third, 2 * third)
+    first_all[pl.ds(pl.multiple_of(me * depth, depth), depth), :] = first_own[...]
+
+    def ordered(ref, offset):
+        return jnp.concatenate(
+            [ref[pl.ds(offset + m, count, stride=depth), :] for m in range(held)], axis=0
+        )
 
     receive(0)
-    whole = first_all[...].reshape(count * depth, nobs)
-
-    def pick(offset):
-        return dot(jnp.where(spot == home + offset, 1.0, 0.0), whole, ((1,), (0,)))
-
-    first_mix = mixing_of(pick(0), pick(held), error)
-    base = pick(2 * held)
+    send(2, 2 * third, count)
+    first_mix = mixing_of(ordered(first_all, 0), ordered(first_all, held), error)
+    base = ordered(first_all, 2 * held)
 
     receive(1)
-    line2 = lax.broadcasted_iota(jnp.int32, (members, deep), 0)
-    spot2 = lax.broadcasted_iota(jnp.int32, (members, deep), 1)
-    home2 = (line2 // held) * FIELDS + line2 % held
-    at = pl.multiple_of(me * (QUARTERS * FIELDS), FIELDS)
+    prior = jnp.concatenate([ordered(patch_all, v * held) for v in range(QUARTERS)], axis=1)
+    shifted = prior + dot(first_mix, prior, ((0,), (0,)))
     perms, lines, marked = [], [[], [], [], []], []
     for v in range(QUARTERS):
-        choose = jnp.where(spot2 == home2 + (v % 2) * held, 1.0, 0.0)
-        values = patch_all[:, v // 2].reshape(deep, LANES)
-        prior = dot(choose, values, ((1,), (0,)))
-        perms.append(prior + dot(first_mix, prior, ((0,), (0,))))
-        own = patch[pl.ds(at + v * FIELDS, FIELDS), :]
+        perms.append(shifted[:, v * LANES : (v + 1) * LANES])
+        own = patch_two[v * FIELDS : (v + 1) * FIELDS, :]
         for f in range(4):
             lines[f].append(own[held + f : held + f + 1])
-        marked.append(mark[pl.ds(at + v * FIELDS, FIELDS), :][0:1])
+        marked.append(mark_two[v * FIELDS : v * FIELDS + 1, :])
     change = patch_plume(perms, *lines)
     sums = sum(jnp.where(m > 0.0, c, 0.0) for c, m in zip(change, marked))
     one = lax.broadcasted_iota(jnp.int32, (SIDE, LANES), 0)
@@ -533,18 +570,28 @@
     mixing = first_mix + second_mix + dot(first_mix, second_mix, ((1,), (0,)))
 
     receive(2)
-    own_in.wait()
-    for r in range(tall):
-        prior = block[:, r, :]
-        mixed[:, r, :] = prior + dot(mixing, prior, ((0,), (0,)))
-    send(4)
-    own_out = pltpu.make_async_copy(members_of(mixed, me), cells_of(out_ref, me), local_sem.at[1])
-    own_out.start()
+    for half in range(wide // LANES):
+        part = slice(half * LANES, (half + 1) * LANES)
+        for r in range(tall):
+            prior = block[:, :, r, part].reshape(members, LANES)
+            fresh = prior + dot(mixing, prior, ((0,), (0,)))
+            mixed[half, :, :, r, :] = fresh.reshape(held, count, LANES)
+        send(4 + half)
+    own_out = [
+        pltpu.make_async_copy(
+            members_of(mixed.at[half], me), half_of(out_ref, me, half), load_sem.at[half]
+        )
+        for half in range(wide // LANES)
+    ]
+    for copy in own_out:
+        copy.start()
     for kind in range(4):
         sent(kind)
-    own_out.wait()
-    receive(4)
-    sent(4)
+    for copy in own_out:
+        copy.wait()
+    for half in range(wide // LANES):
+        receive(4 + half)
+        sent(4 + half)
 
 
 def patch_device(count, perm, start, top, porosity, well, cells, observed, error, noise):
@@ -553,54 +600,68 @@
     members = held * count
     wide = cols // ((count * SIDE) // rows)
     error = error.reshape(1, nobs)
-    operands = (perm, start, top, porosity, well, cells, observed, error, noise)
-    local = [
-        (pltpu.SMEM if x is cells else pltpu.VMEM)(x.shape, x.dtype) for x in operands
-    ]
+    maps = (perm, start, top, porosity, well, cells)
+    rest = (observed, error, noise)
     vmem = pl.BlockSpec(memory_space=pltpu.VMEM)
-    grant = 32 * 1024 * 1024
+    anywhere = pl.BlockSpec(memory_space=pl.ANY)
+    grant = 60 * 1024 * 1024
+    depth = 4 * held
+    group = QUARTERS * FIELDS
+    kinds = 4 + wide // LANES
 
     def scratch(*shape):
         return pltpu.VMEM(shape, jnp.float32)
 
     found = [
-        (4 * held, nobs),
-        (count, QUARTERS // 2, 2 * held, LANES),
-        (count * QUARTERS * FIELDS, LANES),
-        (count * QUARTERS * FIELDS, LANES),
+        (count * group, LANES),
+        (count * group, LANES),
+        (count * depth, LANES),
+        (group, LANES),
+        (group, LANES),
     ]
     gathered = pl.pallas_call(
         functools.partial(local_kernel, count),
         out_shape=[jax.ShapeDtypeStruct(shape, jnp.float32) for shape in found],
-        in_specs=[pl.BlockSpec(memory_space=pl.ANY)] * len(operands),
+        in_specs=[anywhere] * len(maps),
         out_specs=[vmem] * len(found),
-        scratch_shapes=local
+        scratch_shapes=[pltpu.VMEM(x.shape, x.dtype) for x in maps[:-1]]
         + [
+            pltpu.SMEM(cells.shape, cells.dtype),
             scratch(cols // LANES, rows * FIELDS, LANES),
-            scratch(count * FIELDS, LANES),
-            pltpu.SemaphoreType.DMA((len(operands),)),
+            scratch(count * group, LANES),
+            scratch(count * group, LANES),
+            pltpu.SemaphoreType.DMA((len(maps),)),
         ],
         compiler_params=pltpu.CompilerParams(vmem_limit_bytes=grant),
-    )(*operands)
+    )(*maps)
     return pl.pallas_call(
         functools.partial(ensemble_kernel, count),
         out_shape=jax.ShapeDtypeStruct(perm.shape, jnp.float32),
-        in_specs=[vmem] * (len(found) + 2),
-        out_specs=vmem,
+        in_specs=[anywhere] * (1 + len(found) + len(rest)),
+        out_specs=anywhere,
         scratch_shapes=[
-            scratch(count, *found[0]),
+            scratch(*found[0]),
             scratch(*found[1]),
+            scratch(*found[3]),
+            scratch(*found[4]),
+        ]
+        + [pltpu.VMEM(x.shape, x.dtype) for x in rest]
+        + [
+            scratch(count * FIELDS, LANES),
+            scratch(depth, nobs),
+            scratch(count * depth, nobs),
+            scratch(count * depth, LANES),
             scratch(nobs, LANES),
-            scratch(members, SIDE, wide),
-            scratch(members, SIDE, wide),
-            pltpu.SemaphoreType.DMA((KINDS, count)),
-            pltpu.SemaphoreType.DMA((KINDS, count)),
-            pltpu.SemaphoreType.DMA((2,)),
+            scratch(held, count, SIDE, wide),
+            scratch(wide // LANES, held, count, SIDE, LANES),
+            pltpu.SemaphoreType.DMA((kinds, count)),
+            pltpu.SemaphoreType.DMA((kinds, count)),
+            pltpu.SemaphoreType.DMA((len(found) + len(rest) + 1,)),
         ],
         compiler_params=pltpu.CompilerParams(
             collective_id=0, has_side_effects=True, vmem_limit_bytes=grant
         ),
-    )(perm, *gathered, error)
+    )(perm, *gathered, *rest)
 
 
 def fits(count, held, rows, cols, nobs):
@@ -610,6 +671,7 @@
         and nobs == LANES
         and nobs == count * SIDE
         and rows % SIDE == 0
+        and cols & (cols - 1) == 0
         and (count * SIDE) % rows == 0
         and cols % ((count * SIDE // rows) * LANES) == 0
     )

time: 61.9 us -> 55.1 us (0.89); the launches traced: 61.6 us -> 54.1 us
  local copies, waits for them, and re-layouts: 7.51 us -> 1.87 us
  Pallas kernels: 54.1 us -> 52.2 us
    unnamed x19 -> x1, local copies, waits for them, and re-layouts: 7.51 us -> 1.87 us
    pallas_call x1, Pallas kernels: 11.6 us -> 8.13 us  [patch_device(): pl.pallas_call(functools.partial(local_kernel, count), out_shape=[jax.Sha...]
    pallas_call x1, Pallas kernels: 42.4 us -> 44 us  [patch_device(): pl.pallas_call(functools.partial(ensemble_kernel, count), out_shape=jax.S...]
where the time goes in v3:
time: 55.1 us; the launch traced here: 54.1 us
  Pallas kernels  52.2 us (95%)
  local copies, waits for them, and re-layouts  1.87 us (3%)
    pallas_call x1, Pallas kernels, patch_device(): pl.pallas_call(functools.partial(ensemble_kernel, count), out_shape=jax.S...  44 us
    pallas_call x1, Pallas kernels, patch_device(): pl.pallas_call(functools.partial(local_kernel, count), out_shape=[jax.Sha...  8.13 us
    unnamed x1, local copies, waits for them, and re-layouts  1.87 us

profile of v3, /device:TPU:9, one launch (start us, length us, event | category | flops | bytes accessed | tf_op | source)
XLA Modules:
  0.0 54.1 jit_solution(10522314983923640677)
XLA Ops:
  0.0 8.1 %shard_map.91 = (f32[512,128]{1,0:T(8,128)}, f32[512,128]{1,0:T(8,128)}, f32[256,128]{1,0:T(8,128)}, f32[32,128]{1,0:T(8,128)}, f32[32,128]{1,0:T(8,128)}) custom-call(f32[4,64,512]{2,1,0:T(8,128)} %perm_ref.1, f32[64,512]{1,0:T(8,128)} %start_hbm.1, f32[64,512]{1,0:T(8,128)} %top_hbm.1, f32[64,512]{1,0:T(8,128)} %porosity_hbm.1, s32[64,512]{1,0:T(8,128)} %well_hbm.1, ...), custom_call_target="tpu_custom_call" | custom-call | tf_op jit(solution)/shard_map/pallas_call | solution.py:622
  8.1 44.0 %shard_map.92 = f32[4,64,512]{2,1,0:T(8,128)} custom-call(f32[4,64,512]{2,1,0:T(8,128)} %perm_ref.1, f32[512,128]{1,0:T(8,128)} %get-tuple-element.10.patch_one_hbm, f32[512,128]{1,0:T(8,128)} %get-tuple-element.11.mark_one_hbm, f32[256,128]{1,0:T(8,128)} %get-tuple-element.12.patch_own, f32[32,128]{1,0:T(8,128)} %get-tuple-element.13.patch_two_hbm, ...), custom_call_target="tpu_custom_call" | custom-call | tf_op jit(solution)/shard_map/pallas_call | solution.py:637
  52.2 1.9 %copy.11 = f32[4,64,512]{2,1,0:T(8,128)} copy(f32[4,64,512]{2,1,0:T(8,128)} %shard_map.92) | data formatting | bytes 1048576

commit v4 on v3

--- a/solution.py
+++ b/solution.py
@@ -355,8 +355,8 @@
         patch_own[at, :] = jnp.concatenate(rows_of, axis=0)
         return carry
 
-    lax.fori_loop(0, count, second_chunk, 0, unroll=2)
-    lax.fori_loop(0, count, first_chunk, 0, unroll=2)
+    lax.fori_loop(0, count, second_chunk, 0, unroll=4)
+    lax.fori_loop(0, count, first_chunk, 0, unroll=4)
     own = pl.ds(pl.multiple_of(me * short[0], FIELDS), short[0])
     patch_two[...] = patch_all_two[own, :]
     mark_two[...] = mark_all_two[own, :]
@@ -495,24 +495,33 @@
     for load in loads:
         load.wait()
     pl.semaphore_wait(barrier, count - 1)
-    third = (count + 1) // 3
     send(1)
-    send(2, 1, third)
 
     group = QUARTERS * FIELDS
 
-    def first_chunk(chunk, carry):
-        at = pl.ds(pl.multiple_of(chunk * group, group), group)
-        total, marks = patch_one[at, :], mark_one[at, :]
-        parts = [total[v * FIELDS : (v + 1) * FIELDS] for v in range(QUARTERS)]
-        marked = [marks[v * FIELDS : (v + 1) * FIELDS] for v in range(QUARTERS)]
-        lines = [[p[held + f : held + f + 1] for p in parts] for f in range(4)]
+    batch = min(8, count)
+
+    def first_batch(index, carry):
+        parts, lines, marked = [], [[], [], [], []], []
+        for v in range(QUARTERS):
+            totals, marks = [], []
+            for i in range(batch):
+                at = pl.multiple_of((index * batch + i) * group + v * FIELDS, FIELDS)
+                totals.append(patch_one[pl.ds(at, FIELDS), :])
+                marks.append(mark_one[pl.ds(at, FIELDS), :])
+            parts.append(jnp.concatenate(totals, axis=0))
+            marked.append(jnp.concatenate(marks, axis=0))
+            for f in range(4):
+                rows_of = [t[held + f : held + f + 1] for t in totals]
+                spread = [jnp.broadcast_to(r, (FIELDS, LANES)) for r in rows_of]
+                lines[f].append(jnp.concatenate(spread, axis=0))
         change = patch_plume(parts, *lines)
         sums = sum(jnp.where(m > 0.0, c, 0.0) for c, m in zip(change, marked))
-        folded[pl.ds(pl.multiple_of(chunk * FIELDS, FIELDS), FIELDS), :] = sums
+        tall_batch = batch * FIELDS
+        folded[pl.ds(pl.multiple_of(index * tall_batch, FIELDS), tall_batch), :] = sums
         return carry
 
-    lax.fori_loop(0, count, first_chunk, 0, unroll=2)
+    lax.fori_loop(0, count // batch, first_batch, 0)
 
     one = lax.broadcasted_iota(jnp.int32, (LANES, nobs), 0)
     two = lax.broadcasted_iota(jnp.int32, (LANES, nobs), 1)
@@ -532,7 +541,7 @@
     )
     first_own[3 * held : 4 * held, :] = jnp.zeros_like(predicted)
     send(0)
-    send(2, third, 2 * third)
+    send(2)
     first_all[pl.ds(pl.multiple_of(me * depth, depth), depth), :] = first_own[...]
 
     def ordered(ref, offset):
@@ -541,7 +550,6 @@
         )
 
     receive(0)
-    send(2, 2 * third, count)
     first_mix = mixing_of(ordered(first_all, 0), ordered(first_all, held), error)
     base = ordered(first_all, 2 * held)
 
@@ -569,12 +577,13 @@
     second_mix = mixing_of(table, base - table / error, error)
     mixing = first_mix + second_mix + dot(first_mix, second_mix, ((1,), (0,)))
 
+    turned = mixing.T
     receive(2)
     for half in range(wide // LANES):
         part = slice(half * LANES, (half + 1) * LANES)
         for r in range(tall):
             prior = block[:, :, r, part].reshape(members, LANES)
-            fresh = prior + dot(mixing, prior, ((0,), (0,)))
+            fresh = prior + dot(turned, prior, ((1,), (0,)))
             mixed[half, :, :, r, :] = fresh.reshape(held, count, LANES)
         send(4 + half)
     own_out = [
@@ -672,6 +681,7 @@
         and nobs == count * SIDE
         and rows % SIDE == 0
         and cols & (cols - 1) == 0
+        and count % min(8, count) == 0
         and (count * SIDE) % rows == 0
         and cols % ((count * SIDE // rows) * LANES) == 0
     )

time: 55.1 us -> 53.4 us (0.969)
  Pallas kernels: 52.2 us -> 50.5 us
    pallas_call x1, Pallas kernels: 8.13 us -> 7.19 us  [patch_device(): pl.pallas_call(functools.partial(local_kernel, count), out_shape=[jax.Sha...]
    pallas_call x1, Pallas kernels: 44 us -> 43.3 us  [patch_device(): pl.pallas_call(functools.partial(ensemble_kernel, count), out_shape=jax.S...]
where the time goes in v4:
time: 53.4 us; the launch traced here: 52.4 us
  Pallas kernels  50.5 us (95%)
  local copies, waits for them, and re-layouts  1.87 us (4%)
    pallas_call x1, Pallas kernels, patch_device(): pl.pallas_call(functools.partial(ensemble_kernel, count), out_shape=jax.S...  43.3 us
    pallas_call x1, Pallas kernels, patch_device(): pl.pallas_call(functools.partial(local_kernel, count), out_shape=[jax.Sha...  7.19 us
    unnamed x1, local copies, waits for them, and re-layouts  1.87 us

profile of v4, /device:TPU:9, one launch (start us, length us, event | category | flops | bytes accessed | tf_op | source)
XLA Modules:
  0.0 52.4 jit_solution(14327462876344431427)
XLA Ops:
  0.0 7.2 %shard_map.91 = (f32[512,128]{1,0:T(8,128)}, f32[512,128]{1,0:T(8,128)}, f32[256,128]{1,0:T(8,128)}, f32[32,128]{1,0:T(8,128)}, f32[32,128]{1,0:T(8,128)}) custom-call(f32[4,64,512]{2,1,0:T(8,128)} %perm_ref.1, f32[64,512]{1,0:T(8,128)} %start_hbm.1, f32[64,512]{1,0:T(8,128)} %top_hbm.1, f32[64,512]{1,0:T(8,128)} %porosity_hbm.1, s32[64,512]{1,0:T(8,128)} %well_hbm.1, ...), custom_call_target="tpu_custom_call" | custom-call | tf_op jit(solution)/shard_map/pallas_call | solution.py:631
  7.2 43.3 %shard_map.92 = f32[4,64,512]{2,1,0:T(8,128)} custom-call(f32[4,64,512]{2,1,0:T(8,128)} %perm_ref.1, f32[512,128]{1,0:T(8,128)} %get-tuple-element.10.patch_one_hbm, f32[512,128]{1,0:T(8,128)} %get-tuple-element.11.mark_one_hbm, f32[256,128]{1,0:T(8,128)} %get-tuple-element.12.patch_own, f32[32,128]{1,0:T(8,128)} %get-tuple-element.13.patch_two_hbm, ...), custom_call_target="tpu_custom_call" | custom-call | tf_op jit(solution)/shard_map/pallas_call | solution.py:646
  50.5 1.9 %copy.11 = f32[4,64,512]{2,1,0:T(8,128)} copy(f32[4,64,512]{2,1,0:T(8,128)} %shard_map.92) | data formatting | bytes 1048576

commit v5 on v4

--- a/solution.py
+++ b/solution.py
@@ -456,7 +456,12 @@
         lax.fori_loop(low, high, step, 0)
 
     def send(kind, low=1, high=count):
-        each(lambda j: transfer(kind, lax.rem(me + j, count), me, j).start(), low, high)
+        def start(turn):
+            by = (turn // 2) * (1 - 2 * (turn % 2))
+            j = count // 2 + by
+            transfer(kind, lax.rem(me + j, count), me, j).start()
+
+        each(start, low, high)
 
     def receive(kind):
         each(lambda j: transfer(kind, me, lax.rem(me + count - j, count), j).wait_recv())
@@ -496,6 +501,7 @@
         load.wait()
     pl.semaphore_wait(barrier, count - 1)
     send(1)
+    send(2, 1, count // 4)
 
     group = QUARTERS * FIELDS
 
@@ -541,7 +547,7 @@
     )
     first_own[3 * held : 4 * held, :] = jnp.zeros_like(predicted)
     send(0)
-    send(2)
+    send(2, count // 4, count)
     first_all[pl.ds(pl.multiple_of(me * depth, depth), depth), :] = first_own[...]
 
     def ordered(ref, offset):
@@ -679,6 +685,7 @@
         and 2 * count * held == LANES
         and nobs == LANES
         and nobs == count * SIDE
+        and count % 4 == 0
         and rows % SIDE == 0
         and cols & (cols - 1) == 0
         and count % min(8, count) == 0

time: 53.4 us -> 57 us (1.067)
  the two profiles are of different devices: /device:TPU:9 before, /device:TPU:0 now
where the time goes in v5:
time: 57 us; the launch traced here: 56.8 us
  Pallas kernels  55 us (96%)
  local copies, waits for them, and re-layouts  1.87 us (3%)
    pallas_call x1, Pallas kernels, patch_device(): pl.pallas_call(functools.partial(ensemble_kernel, count), out_shape=jax.S...  47.8 us
    pallas_call x1, Pallas kernels, patch_device(): pl.pallas_call(functools.partial(local_kernel, count), out_shape=[jax.Sha...  7.18 us
    unnamed x1, local copies, waits for them, and re-layouts  1.87 us

profile of v5, /device:TPU:0, one launch (start us, length us, event | category | flops | bytes accessed | tf_op | source)
XLA Modules:
  0.0 56.8 jit_solution(3424417645225048551)
XLA Ops:
  0.0 7.2 %shard_map.91 = (f32[512,128]{1,0:T(8,128)}, f32[512,128]{1,0:T(8,128)}, f32[256,128]{1,0:T(8,128)}, f32[32,128]{1,0:T(8,128)}, f32[32,128]{1,0:T(8,128)}) custom-call(f32[4,64,512]{2,1,0:T(8,128)} %perm_ref.1, f32[64,512]{1,0:T(8,128)} %start_hbm.1, f32[64,512]{1,0:T(8,128)} %top_hbm.1, f32[64,512]{1,0:T(8,128)} %porosity_hbm.1, s32[64,512]{1,0:T(8,128)} %well_hbm.1, ...), custom_call_target="tpu_custom_call" | custom-call | tf_op jit(solution)/shard_map/pallas_call | solution.py:637
  7.2 47.8 %shard_map.92 = f32[4,64,512]{2,1,0:T(8,128)} custom-call(f32[4,64,512]{2,1,0:T(8,128)} %perm_ref.1, f32[512,128]{1,0:T(8,128)} %get-tuple-element.10.patch_one_hbm, f32[512,128]{1,0:T(8,128)} %get-tuple-element.11.mark_one_hbm, f32[256,128]{1,0:T(8,128)} %get-tuple-element.12.patch_own, f32[32,128]{1,0:T(8,128)} %get-tuple-element.13.patch_two_hbm, ...), custom_call_target="tpu_custom_call" | custom-call | tf_op jit(solution)/shard_map/pallas_call | solution.py:652
  55.0 1.9 %copy.11 = f32[4,64,512]{2,1,0:T(8,128)} copy(f32[4,64,512]{2,1,0:T(8,128)} %shard_map.92) | data formatting | bytes 1048576
